TPU v7x, 512 devices: a whole 4x8x8 slice. The times are simulated.
512 devices in a mesh: leaf: 128 (over y, z, core), probe: 4 (over x).
Axes of the slice: x: 4, y: 8, z: 8, core: 2. Of those that a mesh axis runs over, the one named last changes fastest.
Arguments:
- points: bfloat16 [262144, 64], P('leaf'), may hold values from -6 to 6
- probes: bfloat16 [262144, 256], P('leaf', 'probe'), may hold values from -6 to 6
- near_list: int32 [1024, 16], P('leaf'), may hold values from 0 to 1023, as said below
- near_count: int32 [1024], P('leaf'), may hold values from 1 to 16, as said below
Outputs:
- samples: float32 [262144, 256], P('leaf', 'probe')
- node_factors: float32 [128, 3, 256, 256], P('leaf')
- root_factor: float32 [256, 256], replicated
Inputs may be any that keep to these rules, and one draw needn't show every extreme that they name: near_list[i, 0] = i; every id lies within 8 boxes of i. `near_count`: the first box of each device has all 16 slots live.
All inputs are finite; a program needn't handle non-finite values.
Results may differ from a plain program's by a relative error of at most 0.0003.
Values may be sent and summed in bfloat16 or wider, within the bound.
No kernel may reach another device: no remote copies, remote signals or barrier semaphores. Data moves between devices by JAX's collectives and lax.ppermute only.
A program may use at most 64 MiB of HBM per device.

v0:
```python
import jax
import jax.numpy as jnp
from jax import lax
from jax.sharding import PartitionSpec as P

LEVELS = 3


def padded(block, sides, width):
    for axis, dim in sides:
        count = lax.axis_size(axis)
        forward = [(i, i + 1) for i in range(count - 1)]
        backward = [(target, source) for source, target in forward]
        low = lax.ppermute(
            lax.slice_in_dim(block, block.shape[dim] - width, None, axis=dim), axis, forward
        )
        high = lax.ppermute(lax.slice_in_dim(block, 0, width, axis=dim), axis, backward)
        block = jnp.concatenate([low, block, high], axis=dim)
    return block


def from_partner(x, axis, bit):
    return lax.ppermute(x, axis, [(i, i ^ 1 << bit) for i in range(lax.axis_size(axis))])


def body(points, probes, near_list, near_count):
    blocks = near_list.shape[0]
    rows = points.shape[0]
    box = rows // blocks
    feats = points.shape[1]
    cols = probes.shape[1]
    rank = cols * lax.axis_size("probe")
    packed = jnp.concatenate([points, probes], axis=1)
    extended = padded(packed, (("leaf", 0),), rows)
    boxes = extended.reshape(3 * blocks, box, feats + cols)
    base = lax.axis_index("leaf") * blocks - blocks
    own = points.reshape(blocks, box, feats)
    own_wide = own.astype(jnp.float32)
    sq_own = jnp.sum(own_wide * own_wide, axis=-1)

    def one_slot(slot, total):
        index = lax.dynamic_index_in_dim(near_list, slot, 1, False) - base
        piece = boxes[index]
        other = piece[:, :, :feats]
        other_wide = other.astype(jnp.float32)
        sq_other = jnp.sum(other_wide * other_wide, axis=-1)
        cross = jnp.einsum("bid,bjd->bij", own, other, preferred_element_type=jnp.float32)
        dist = sq_own[:, :, None] + sq_other[:, None, :] - 2.0 * cross
        live = (slot < near_count).astype(jnp.float32)
        tile = jnp.exp(-dist / (feats / 2.0)) * live[:, None, None]
        columns = piece[:, :, feats:].astype(jnp.float32)
        return total + jnp.einsum(
            "bij,bjr->bir",
            tile,
            columns,
            precision=lax.Precision.HIGHEST,
            preferred_element_type=jnp.float32,
        )

    start_total = jnp.zeros((blocks, box, cols), jnp.float32)
    samples = lax.fori_loop(0, near_list.shape[1], one_slot, start_total).reshape(rows, cols)
    whole = lax.all_gather(samples, "probe", axis=1, tiled=True)
    gram = jnp.dot(
        whole.T, whole, precision=lax.Precision.HIGHEST, preferred_element_type=jnp.float32
    )
    eye = jnp.eye(rank, dtype=jnp.float32)
    running = gram
    factors = []
    for level in range(LEVELS):
        running = running + from_partner(running, "leaf", level)
        factors.append(jnp.linalg.cholesky(running / (rows * 2 ** (level + 1)) + eye))
    node_factors = jnp.stack(factors, axis=0)[None]
    leaf_count = lax.axis_size("leaf")
    everything = lax.psum(gram, "leaf")
    root_factor = jnp.linalg.cholesky(everything / (rows * leaf_count) + eye)
    return (samples, node_factors, root_factor)


def solution(mesh):
    return jax.shard_map(
        body,
        mesh=mesh,
        in_specs=(P("leaf", None), P("leaf", "probe"), P("leaf", None), P("leaf")),
        out_specs=(P("leaf", "probe"), P("leaf", None, None, None), P()),
        check_vma=False,
    )
```

profile of v0, /device:TPU:1, one launch (start us, length us, event | category | flops | bytes accessed | tf_op | source)
XLA Modules:
  0.0 455.6 jit_solution(1807203300164821421)
XLA Ops:
  7.2 1.0 constant_dynamic-update-slice_fusion.1
  8.2 1.0 constant_dynamic-update-slice_fusion
  9.2 8.8 %collective-permute-start.1 = (bf16[2048,128]{0,1:T(8,128)(2,1)S(1)}, bf16[2048,128]{0,1:T(8,128)(2,1)S(1)}, u32[]{:S(2)}, u32[]{:S(2)}) collective-permute-start(bf16[2048,128]{0,1:T(8,128)(2,1)S(1)} %constant_dynamic-update-slice_fusion), channel_id=1, source_target_pairs={{4,0},{8,4},{12,8},{16,12},{20,16},{24,20},{28,24},{32,28},{36,32}... | collective-permute-start | bytes 1572872 | tf_op jit(solution)/shard_map/ppermute | solution.py:17
  17.9 1.9 collective-permute-start
  19.9 1.2 copy.20
  21.9 1.0 multiply_reduce_fusion.1
  22.9 3.0 collective-permute-done
  26.0 1.3 pad_maximum_fusion
  27.2 1.9 copy.19
  29.2 58.5 %while.14 = (s32[]{:T(128)}, f32[8,256,64]{1,2,0:T(8,128)S(1)}, f32[8,256]{1,0:T(8,128)S(1)}, s32[8,16]{0,1:T(8,128)S(1)}, s32[]{:T(128)}, /*index=5*/bf16[24,25...) while((s32[]{:T(128)}, f32[8,256,64]{1,2,0:T(8,128)S(1)}, ...), condition=%wide.region_3.4_spmd.clone, body=%wide.region_1.3_spmd.clone.sunk | while | flops 473562176 | bytes 7893347 | solution.py:61
  30.7 2.1 fusion.63
  34.3 2.1 fusion.63
  38.0 2.1 fusion.63
  41.7 2.1 fusion.63
  45.3 2.1 fusion.63
  49.0 2.1 fusion.63
  52.6 2.1 fusion.63
  56.3 2.1 fusion.63
  59.9 2.1 fusion.63
  63.6 2.1 fusion.63
  67.2 2.1 fusion.63
  70.9 2.1 fusion.63
  74.5 2.1 fusion.63
  78.2 2.1 fusion.63
  81.9 2.1 fusion.63
  85.5 2.1 fusion.63
  88.5 40.6 %all-gather.2.cloned.1.call-done = f32[2048,256]{0,1:T(8,128)} async-done(((f32[2048,64]{0,1:T(8,128)}), f32[2048,256]{0,1:T(8,128)}) %all-gather.2.cloned.1.call-update) | async-done | bytes 2097168 | tf_op jit(solution)/shard_map/all_gather | solution.py:62
  129.1 4.1 fusion.38
  133.2 2.6 collective-permute-start.2
  135.8 1.1 collective-permute-done.2
  137.9 3.8 collective-permute-start.3
  141.8 11.7 %cholesky.214 = f32[128,128]{1,0:T(8,128)S(1)} custom-call(f32[128,128]{1,0:T(8,128)S(1)} %cholesky.346), custom_call_target="Cholesky" | custom-call | tf_op jit(solution)/shard_map/jit(cholesky)/cholesky | solution.py:71
  153.5 9.8 %custom-call.12 = f32[1,128,128]{1,2,0:T(8,128)S(1)} custom-call(f32[1,128,128]{2,1,0:T(8,128)S(1)} %get-tuple-element.214), custom_call_target="InvertDiagBlocksLowerTriangular" | custom-call | tf_op jit(solution)/shard_map/jit(cholesky)/cholesky | solution.py:71
  163.8 11.7 %cholesky.231 = f32[128,128]{1,0:T(8,128)S(1)} custom-call(f32[128,128]{1,0:T(8,128)S(1)} %convolution_subtract_fusion.3), custom_call_target="Cholesky" | custom-call | tf_op jit(solution)/shard_map/jit(cholesky)/cholesky | solution.py:71
  177.6 153.0 %all-reduce.3.cloned.1.call-done = f32[256,256]{0,1:T(8,128)} async-done(((f32[256,256]{0,1:T(8,128)}), f32[256,256]{0,1:T(8,128)}) %all-reduce.3.cloned.1.call-update) | async-done | bytes 262160 | tf_op jit(solution)/shard_map/psum | solution.py:74
  330.6 1.0 convert_add_fusion
  331.8 1.0 fusion.22
  332.8 11.9 %cholesky.316 = f32[128,128]{1,0:T(8,128)S(1)} custom-call(f32[128,128]{1,0:T(8,128)S(1)} %cholesky.355), custom_call_target="Cholesky" | custom-call | tf_op jit(solution)/shard_map/jit(cholesky)/cholesky | solution.py:75
  344.7 9.8 %custom-call.15 = f32[1,128,128]{1,2,0:T(8,128)S(1)} custom-call(f32[1,128,128]{2,1,0:T(8,128)S(1)} %get-tuple-element.210), custom_call_target="InvertDiagBlocksLowerTriangular" | custom-call | tf_op jit(solution)/shard_map/jit(cholesky)/cholesky | solution.py:75
  355.0 11.7 %cholesky.333 = f32[128,128]{1,0:T(8,128)S(1)} custom-call(f32[128,128]{1,0:T(8,128)S(1)} %convolution_subtract_fusion), custom_call_target="Cholesky" | custom-call | tf_op jit(solution)/shard_map/jit(cholesky)/cholesky | solution.py:75
  369.7 11.9 %cholesky.248 = f32[128,128]{1,0:T(8,128)S(1)} custom-call(f32[128,128]{1,0:T(8,128)S(1)} %cholesky.349), custom_call_target="Cholesky" | custom-call | tf_op jit(solution)/shard_map/jit(cholesky)/cholesky | solution.py:71
  381.6 5.4 %collective-permute-start.4 = (f32[256,256]{0,1:T(8,128)S(1)}, f32[256,256]{0,1:T(8,128)S(1)}, u32[]{:S(2)}, u32[]{:S(2)}) collective-permute-start(f32[256,256]{0,1:T(8,128)S(1)} %get-tuple-element.206), channel_id=1, source_target_pairs={{0,16},{4,20},{8,24},{12,28},{16,0},{20,4},{24,8},{28,12},{32,48},... | collective-permute-start | bytes 786440 | tf_op jit(solution)/shard_map/ppermute | solution.py:23
  387.1 9.8 %custom-call.13 = f32[1,128,128]{1,2,0:T(8,128)S(1)} custom-call(f32[1,128,128]{2,1,0:T(8,128)S(1)} %get-tuple-element.218), custom_call_target="InvertDiagBlocksLowerTriangular" | custom-call | tf_op jit(solution)/shard_map/jit(cholesky)/cholesky | solution.py:71
  397.4 11.7 %cholesky.265 = f32[128,128]{1,0:T(8,128)S(1)} custom-call(f32[128,128]{1,0:T(8,128)S(1)} %convolution_subtract_fusion.2), custom_call_target="Cholesky" | custom-call | tf_op jit(solution)/shard_map/jit(cholesky)/cholesky | solution.py:71
  411.5 11.7 %cholesky.282 = f32[128,128]{1,0:T(8,128)S(1)} custom-call(f32[128,128]{1,0:T(8,128)S(1)} %cholesky.352), custom_call_target="Cholesky" | custom-call | tf_op jit(solution)/shard_map/jit(cholesky)/cholesky | solution.py:71
  423.2 10.0 %custom-call.14 = f32[1,128,128]{1,2,0:T(8,128)S(1)} custom-call(f32[1,128,128]{2,1,0:T(8,128)S(1)} %get-tuple-element.222), custom_call_target="InvertDiagBlocksLowerTriangular" | custom-call | tf_op jit(solution)/shard_map/jit(cholesky)/cholesky | solution.py:71
  433.8 11.7 %cholesky.299 = f32[128,128]{1,0:T(8,128)S(1)} custom-call(f32[128,128]{1,0:T(8,128)S(1)} %convolution_subtract_fusion.1), custom_call_target="Cholesky" | custom-call | tf_op jit(solution)/shard_map/jit(cholesky)/cholesky | solution.py:71
  447.6 0.9 maximum_bitcast_fusion
  (153 shorter events, 32.3 us)
Async XLA Ops:
  7.2 122.0 %all-gather.2.cloned.1.call-start = ((), (), s32[]{:S(2)}) async-start(), calls=%async_computation | async-start | bytes 2621440 | tf_op jit(solution)/shard_map/all_gather | solution.py:62
  9.2 13.8 %collective-permute-start.1 = (bf16[2048,128]{0,1:T(8,128)(2,1)S(1)}, bf16[2048,128]{0,1:T(8,128)(2,1)S(1)}, u32[]{:S(2)}, u32[]{:S(2)}) collective-permute-start(bf16[2048,128]{0,1:T(8,128)(2,1)S(1)} %constant_dynamic-update-slice_fusion), channel_id=1, source_target_pairs={{4,0},{8,4},{12,8},{16,12},{20,16},{24,20},{28,24},{32,28},{36,32}... | collective-permute-start | bytes 1572872 | tf_op jit(solution)/shard_map/ppermute | solution.py:17
  17.9 8.0 %collective-permute-start = (bf16[2048,128]{0,1:T(8,128)(2,1)S(1)}, bf16[2048,128]{0,1:T(8,128)(2,1)S(1)}, u32[]{:S(2)}, u32[]{:S(2)}) collective-permute-start(bf16[2048,128]{0,1:T(8,128)(2,1)S(1)} %constant_dynamic-update-slice_fusion), channel_id=1, source_target_pairs={{0,4},{4,8},{8,12},{12,16},{16,20},{20,24},{24,28},{28,32},{32,36}... | collective-permute-start | bytes 1572872 | tf_op jit(solution)/shard_map/ppermute | solution.py:14
  27.2 1.9 copy-start.1
  133.2 3.8 copy-start
  133.2 3.7 collective-permute-start.2
  137.0 193.6 %all-reduce.3.cloned.1.call-start = ((), (), s32[]{:S(2)}) async-start(), calls=%async_computation.1 | async-start | bytes 524288 | tf_op jit(solution)/shard_map/psum | solution.py:74
  137.9 231.5 %collective-permute-start.3 = (f32[256,256]{0,1:T(8,128)S(1)}, f32[256,256]{0,1:T(8,128)S(1)}, u32[]{:S(2)}, u32[]{:S(2)}) collective-permute-start(f32[256,256]{0,1:T(8,128)S(1)} %get-tuple-element.204), channel_id=1, source_target_pairs={{0,8},{4,12},{8,0},{12,4},{16,24},{20,28},{24,16},{28,20},{32,40},... | collective-permute-start | bytes 786440 | tf_op jit(solution)/shard_map/ppermute | solution.py:23
  381.6 29.6 %collective-permute-start.4 = (f32[256,256]{0,1:T(8,128)S(1)}, f32[256,256]{0,1:T(8,128)S(1)}, u32[]{:S(2)}, u32[]{:S(2)}) collective-permute-start(f32[256,256]{0,1:T(8,128)S(1)} %get-tuple-element.206), channel_id=1, source_target_pairs={{0,16},{4,20},{8,24},{12,28},{16,0},{20,4},{24,8},{28,12},{32,48},... | collective-permute-start | bytes 786440 | tf_op jit(solution)/shard_map/ppermute | solution.py:23
Sparse Core Ops, SparseCore 0:
  88.7 40.4 all-gather.1
  141.6 188.9 all-reduce.2
where the time goes:
time: 460 us; the launch traced here: 456 us
  waiting for transfers between devices  199 us (43%)
  other arithmetic  149 us (32%)
  matrix products  47.2 us (10%)
  starting transfers between devices  22.6 us (5%)
  between operations  19.9 us (4%)
  local copies, waits for them, and re-layouts  17.7 us (4%)
    psum x1, waiting for transfers between devices, body(): everything = lax.psum(gram, 'leaf')  153 us
    another operation x18, other arithmetic, body(): jnp.linalg.cholesky(running / (rows * 2 ** (level + 1)) + eye)  102 us
    all_gather x1, waiting for transfers between devices, body(): whole = lax.all_gather(samples, 'probe', axis=1, tiled=True)  40.6 us
    dot_general x16, matrix products, one_slot(): jnp.einsum('bij,bjr->bir', tile, columns, precision=lax.Precision.HIGHEST...  34.2 us
    another operation x6, other arithmetic, body(): root_factor = jnp.linalg.cholesky(everything / (rows * leaf_count) + eye)  34.1 us
    ppermute x3, starting transfers between devices, from_partner(): lax.ppermute(x, axis, [(i, i ^ 1 << bit) for i in range(lax.axis_size(axi...  11.8 us
    gather x16, local copies, waits for them, and re-layouts, one_slot(): piece = boxes[index]  10.4 us
  transfers between devices with their start and end apart: 7, of which 4 were waited for; matrix products, arithmetic and copies ran while one was open for 21% of the time, Pallas kernels for 0%

commit v1 on v0

v1 whole, which is shorter than its diff:
```python
import functools

import jax
import jax.numpy as jnp
from jax import lax
from jax.experimental import pallas as pl
from jax.experimental.pallas import tpu as pltpu
from jax.sharding import Mesh, PartitionSpec as P

LEVELS = 3
BLOCKS = 8
BOX = 256
SLOTS = 16
STEPS = BLOCKS * SLOTS // 2 + 16
BF = jnp.bfloat16
F = jnp.float32
NN = (((1,), (0,)), ((), ()))
NT = (((1,), (1,)), ((), ()))
TN = (((0,), (0,)), ((), ()))
LOG2E_OVER_32 = 1.4426950408889634 / 32.0
LIMIT = 48 << 20
VM = pl.BlockSpec(memory_space=pltpu.VMEM)
SM = pl.BlockSpec(memory_space=pltpu.SMEM)


def dot(a, b, dims):
    return lax.dot_general(a, b, dims, preferred_element_type=F)


def squares(x):
    wide = x.astype(F)
    wide = wide * wide
    high = wide.astype(BF)
    return high, (wide - high.astype(F)).astype(BF)


def split3(x):
    h = x.astype(BF)
    r = x - h.astype(F)
    m = r.astype(BF)
    return h, m, (r - m.astype(F)).astype(BF)


def list_steps(offsets, base, list_ref, count_ref, ids):
    for e in range(2):
        for r in range(3):
            ids[r, e] = 0
        ids[3, e] = 1
        ids[4, e] = 1

    def box_list(b, n):
        def one(s, carry):
            n, half = carry
            j = list_ref[b, s] - base
            hit = None
            place = jnp.int32(0)
            for q, off in enumerate(offsets):
                inside = jnp.logical_and(j >= off, j < off + BLOCKS)
                place = jnp.where(inside, j - off + BLOCKS * q, place)
                hit = inside if hit is None else jnp.logical_or(hit, inside)

            @pl.when(jnp.logical_and(hit, half == 0))
            def _():
                ids[0, n] = b
                ids[1, n] = place
                ids[2, n] = place
                ids[3, n] = 0
                ids[4, n] = 1

            @pl.when(jnp.logical_and(hit, half == 1))
            def _():
                ids[2, n - 1] = place
                ids[4, n - 1] = 0

            h = hit.astype(jnp.int32)
            return n + jnp.where(half == 0, h, 0), half ^ h

        n, _ = lax.fori_loop(0, count_ref[b], one, (n, jnp.int32(0)))
        return n

    n = lax.fori_loop(0, BLOCKS, box_list, jnp.int32(2))
    for e in range(2):
        for r in range(3):
            ids[r, n + e] = 0
        ids[3, n + e] = 1
        ids[4, n + e] = 1
    return n


def tiles_kernel(offsets, first, base_ref, list_ref, count_ref, own_ref, *rest):
    count = len(offsets)
    source_refs, rest = rest[:count], rest[count:]
    if first:
        total = rest[0]
        rest = rest[1:]
    else:
        previous, samples_ref, send_ref = rest[:3]
        total = rest[-1]
        rest = rest[3:-1]
    sq_own, sq_other, left, boxes, ids, cross, parts = rest
    points_lane = lax.broadcasted_iota(jnp.int32, (BOX, 128), 1) >= 64
    ones_row = jnp.where(lax.broadcasted_iota(jnp.int32, (8, 128), 1) >= 64, 1.0, 0.0).astype(BF)
    ones_all = jnp.where(lax.broadcasted_iota(jnp.int32, (128, 128), 0) >= 64, 1.0, 0.0).astype(BF)
    n = list_steps(offsets, base_ref[0], list_ref, count_ref, ids)
    for b in range(BLOCKS):
        x = own_ref[b]
        h, l = squares(x)
        sq_own[b] = dot(h, ones_all, NN) + dot(l, ones_all, NN)
        left[b] = jnp.where(points_lane, x.astype(F) * 2.0, 0.0).astype(BF)
        total[b] = jnp.zeros((BOX, 128), F) if first else previous[b]
    for q in range(count):
        for b in range(BLOCKS):
            x = source_refs[q][b]
            boxes[BLOCKS * q + b] = x
            h, l = squares(x)
            sq_other[BLOCKS * q + b] = dot(ones_row, h, NT) + dot(ones_row, l, NT)
    cross[...] = jnp.zeros_like(cross)
    parts[...] = jnp.zeros_like(parts)

    def entry(t):
        return tuple(ids[r, t] for r in range(5))

    def step(t, _):
        i, a, b, _, _ = entry(t - 2)
        columns = jnp.concatenate([boxes[a], boxes[b], boxes[a], boxes[b]], axis=0)
        total[i] = total[i] + dot(parts[...], columns, NN)
        i, a, b, dead_a, dead_b = entry(t - 1)
        own_sq = sq_own[i]
        own_sq = jnp.concatenate([own_sq, own_sq], axis=1)
        x = cross[...]
        high, low = [], []
        for c, (slot, dead) in enumerate(((a, dead_a), (b, dead_b))):
            row = sq_other[slot][0:1, :] + dead.astype(F) * 1e30
            tile = jnp.exp2((x[:, BOX * c:BOX * c + BOX] - row - own_sq) * LOG2E_OVER_32)
            h = tile.astype(BF)
            high.append(h)
            low.append((tile - h.astype(F)).astype(BF))
        parts[...] = jnp.concatenate(high + low, axis=1)
        i, a, b, _, _ = entry(t)
        cross[...] = dot(left[i], jnp.concatenate([boxes[a], boxes[b]], axis=0), NT)
        return 0

    lax.fori_loop(2, n + 2, step, 0)
    if not first:
        for b in range(BLOCKS):
            samples_ref[BOX * b:BOX * b + BOX, :] = total[b][:, :64]
        for p in range(BLOCKS // 2):
            send_ref[p] = jnp.concatenate([total[2 * p][:, :64], total[2 * p + 1][:, :64]], axis=1)


def tiles(base, near_list, near_count, own, sources, offsets, previous=None):
    first = previous is None
    count = len(sources)
    args = [base, near_list, near_count, own] + list(sources)
    totals = jax.ShapeDtypeStruct((BLOCKS, BOX, 128), F)
    if first:
        out_shape, out_specs = totals, VM
    else:
        args.append(previous)
        out_shape = (
            jax.ShapeDtypeStruct((BLOCKS * BOX, 64), F),
            jax.ShapeDtypeStruct((BLOCKS // 2, BOX, 128), F),
        )
        out_specs = (VM, VM)
    scratch = [
        pltpu.VMEM((BLOCKS, BOX, 128), F),
        pltpu.VMEM((BLOCKS * count, 8, BOX), F),
        pltpu.VMEM((BLOCKS, BOX, 128), BF),
        pltpu.VMEM((BLOCKS * count, BOX, 128), BF),
        pltpu.SMEM((5, STEPS), jnp.int32),
        pltpu.VMEM((BOX, 2 * BOX), F),
        pltpu.VMEM((BOX, 4 * BOX), BF),
    ]
    if not first:
        scratch.append(pltpu.VMEM((BLOCKS, BOX, 128), F))
    return pl.pallas_call(
        functools.partial(tiles_kernel, offsets, first),
        out_shape=out_shape,
        in_specs=[SM] * 3 + [VM] * (len(args) - 3),
        out_specs=out_specs,
        scratch_shapes=scratch,
        compiler_params=pltpu.CompilerParams(vmem_limit_bytes=LIMIT),
        cost_estimate=pl.CostEstimate(
            flops=60 * 4 * BOX * BOX * 128 * 2, bytes_accessed=4 << 20, transcendentals=60 * BOX * BOX
        ),
    )(*args)


def gram_kernel(columns_ref, out_ref):
    s = jnp.concatenate(
        [
            jnp.concatenate([columns_ref[q][:, 64 * h:64 * h + 64] for q in range(4)], axis=1)
            for h in range(2)
        ],
        axis=0,
    )
    h, m, l = split3(s)
    left = jnp.concatenate([h, h, m, h, m, l], axis=0)
    right = jnp.concatenate([h, m, h, l, m, h], axis=0)
    g = dot(left, right, TN)
    out_ref[0:128, :] = g[0:128, 0:128]
    out_ref[128:256, :] = g[0:128, 128:256]
    out_ref[256:384, :] = g[128:256, 128:256]


def gram(columns):
    return pl.pallas_call(
        gram_kernel,
        out_shape=jax.ShapeDtypeStruct((384, 128), F),
        in_specs=[VM],
        out_specs=VM,
        compiler_params=pltpu.CompilerParams(vmem_limit_bytes=LIMIT),
    )(columns)


def panel_step(rows, off, width):
    n = len(rows)
    lanes = range(width // 128)
    sub = lax.broadcasted_iota(jnp.int32, (8, 128), 0)
    part = [[[r[8 * g:8 * g + 8, 128 * q:128 * q + 128] for q in lanes] for g in range(4)] for r in rows]
    for s in range(4):
        at = off + 8 * s
        cols = [
            [
                None if g < s else [
                    jnp.broadcast_to(part[b][g][0][:, at + j:at + j + 1], (8, 128)) for j in range(8)
                ]
                for g in range(4)
            ]
            for b in range(n)
        ]
        scale = [None] * n
        for j in range(8):
            for b in range(n):
                here = cols[b][s]
                pivot = jnp.broadcast_to(here[j][j:j + 1, :], (8, 128))
                inverse = 1.0 / pivot
                root = lax.rsqrt(pivot)
                scale[b] = root if j == 0 else jnp.where(sub == j, root, scale[b])
                ratio = [
                    None if l <= j else jnp.broadcast_to(here[l][j:j + 1, :], (8, 128)) * inverse
                    for l in range(8)
                ]
                row = [jnp.broadcast_to(part[b][s][q][j:j + 1, :], (8, 128)) * inverse for q in lanes]
                for g in range(s, 4):
                    c = cols[b][g][j]
                    for l in range(j + 1, 8):
                        cols[b][g][l] = cols[b][g][l] - c * ratio[l]
                    if g == s:
                        c = jnp.where(sub > j, c, 0.0)
                    part[b][g] = [part[b][g][q] - c * row[q] for q in lanes]
        for b in range(n):
            part[b][s] = [v * scale[b] for v in part[b][s]]
    return [jnp.concatenate([jnp.concatenate(v, axis=1) for v in p], axis=0) for p in part]


def factor(n, work, upper):
    for half in range(2):
        c0 = 128 * half
        for k in range(4):
            r0 = c0 + 32 * k
            rows = panel_step([work[b, r0:r0 + 32, c0:256] for b in range(n)], 32 * k, 256 - c0)
            for b in range(n):
                upper[b, r0:r0 + 32, c0:256] = rows[b]
            lo = r0 + 32
            if lo == 256:
                break
            for b in range(n):
                h, m, l = split3(rows[b])
                left = jnp.concatenate([h, h, m, h, m, l], axis=0)
                right = jnp.concatenate([h, m, h, l, m, h], axis=0)
                work[b, lo:256, c0:256] = work[b, lo:256, c0:256] - dot(left, right, TN)[lo - c0:, :]


def factor_kernel(scales, slices_ref, nodes_ref, root_ref, work, upper):
    n = len(scales)
    ri = lax.broadcasted_iota(jnp.int32, (128, 128), 0)
    ci = lax.broadcasted_iota(jnp.int32, (128, 128), 1)
    eye = jnp.where(ri == ci, 1.0, 0.0)
    for b in range(n):
        tri = jnp.concatenate([slices_ref[r, b] for r in range(8)], axis=0) * scales[b]
        work[b, 0:128, 0:128] = tri[0:128] + eye
        work[b, 0:128, 128:256] = tri[128:256]
        work[b, 128:256, 0:128] = jnp.zeros((128, 128), F)
        work[b, 128:256, 128:256] = tri[256:384] + eye
        upper[b, 128:256, 0:128] = jnp.zeros((128, 128), F)
    factor(n, work, upper)
    rows = lax.broadcasted_iota(jnp.int32, (256, 256), 0)
    cols = lax.broadcasted_iota(jnp.int32, (256, 256), 1)
    for b in range(n):
        low = jnp.where(rows >= cols, upper[b].T, 0.0)
        if b < LEVELS:
            nodes_ref[0, b] = low
        else:
            root_ref[...] = low


def factors(slices, scales):
    n = len(scales)
    return pl.pallas_call(
        functools.partial(factor_kernel, scales),
        out_shape=(
            jax.ShapeDtypeStruct((1, LEVELS, 256, 256), F),
            jax.ShapeDtypeStruct((256, 256), F),
        ),
        in_specs=[VM],
        out_specs=(VM, VM),
        scratch_shapes=[pltpu.VMEM((n, 256, 256), F)] * 2,
        compiler_params=pltpu.CompilerParams(vmem_limit_bytes=LIMIT),
    )(slices)


def exchange(x, axes):
    return lax.all_to_all(x, axes, 0, 0)


def to_all(x, axes, n):
    return exchange(jnp.broadcast_to(x[None], (n,) + x.shape), axes)


def body(points, probes, near_list, near_count):
    leaf = ("y", "z", "c")
    size = lax.axis_size(leaf)
    rows = points.shape[0]
    packed = jnp.concatenate([probes, points], axis=1)
    up = [(i, i + 1) for i in range(size - 1)]
    below = lax.ppermute(packed, leaf, up).reshape(BLOCKS, BOX, 128)
    above = lax.ppermute(packed, leaf, [(b, a) for a, b in up]).reshape(BLOCKS, BOX, 128)
    own = packed.reshape(BLOCKS, BOX, 128)
    base = (lax.axis_index(leaf) * BLOCKS).astype(jnp.int32).reshape(1)
    partial = tiles(base, near_list, near_count, own, [own], [0])
    samples, send = tiles(
        base, near_list, near_count, own, [below, above], [-BLOCKS, BLOCKS], partial
    )
    columns = exchange(send, "x")
    pieces = gram(columns).reshape(8, 48, 128)
    level1 = jnp.sum(exchange(pieces, ("c", "x")), axis=0)
    along_z = to_all(level1, "z", 8)
    z = lax.axis_index("z")
    pair = lax.dynamic_slice_in_dim(along_z, z // 2 * 2, 2, 0)
    four = lax.dynamic_slice_in_dim(along_z, z // 4 * 4, 4, 0)
    level2 = jnp.sum(pair, axis=0)
    level3 = jnp.sum(four, axis=0)
    along_y = to_all(jnp.sum(along_z, axis=0), "y", 8)
    root = jnp.sum(along_y, axis=0)
    slices = to_all(jnp.stack([level1, level2, level3, root]), ("c", "x"), 8)
    scales = [1.0 / (rows * 2 ** (l + 1)) for l in range(LEVELS)] + [1.0 / (rows * size)]
    node_factors, root_factor = factors(slices, scales)
    return samples, node_factors, root_factor


def solution(mesh):
    fine = Mesh(mesh.devices.reshape(8, 8, 2, 4), ("y", "z", "c", "x"))
    leaf = ("y", "z", "c")
    return jax.shard_map(
        body,
        mesh=fine,
        in_specs=(P(leaf, None), P(leaf, "x"), P(leaf, None), P(leaf)),
        out_specs=(P(leaf, "x"), P(leaf, None, None, None), P()),
        check_vma=False,
    )
```

time: 460 us -> 132 us (0.29)
  waiting for transfers between devices: 199 us -> 19.8 us
  other arithmetic: 149 us -> 0.08 us
  matrix products: 47.2 us -> 0 us
  blocking collectives: 0 us -> 41 us
  Pallas kernels: 0 us -> 35.3 us
  between operations: 19.9 us -> 0.8 us
  local copies, waits for them, and re-layouts: 17.7 us -> 7.49 us
  starting transfers between devices: 22.6 us -> 27.5 us
    psum x1 -> x0, waiting for transfers between devices: 153 us -> none  [body(): everything = lax.psum(gram, 'leaf')]
    another operation x27 -> x1, other arithmetic: 137 us -> 0.01 us  [body(): slices = to_all(jnp.stack([level1, level2, level3, root]), ('c', 'x'), 8)]
    dot_general x33 -> x0, matrix products: 45.3 us -> none  [the longest x16 34.2 us: one_slot(): jnp.einsum('bij,bjr->bir', tile, columns, precision=lax.Precision.HIGHEST...]
    all_to_all x0 -> x3, blocking collectives: none -> 41 us  [exchange(): return lax.all_to_all(x, axes, 0, 0)]
    all_gather x1 -> x0, waiting for transfers between devices: 40.6 us -> none  [body(): whole = lax.all_gather(samples, 'probe', axis=1, tiled=True)]
    pallas_call x0 -> x4, Pallas kernels: none -> 35.3 us  [the longest x2 22.7 us: tiles(): pl.pallas_call(functools.partial(tiles_kernel, offsets, first), out_shape...]
    all_to_all x0 -> x2, waiting for transfers between devices: none -> 19.8 us  [exchange(): return lax.all_to_all(x, axes, 0, 0)]
    all_to_all x0 -> x2, starting transfers between devices: none -> 17.4 us  [exchange(): return lax.all_to_all(x, axes, 0, 0)]
  transfers between devices with their start and end apart: 7 -> 4, of which waited for: 4 -> 2; matrix products, arithmetic and copies ran while one was open for 21% -> 1% of each run, Pallas kernels for 0% -> 8%
where the time goes in v1:
time: 132 us
  blocking collectives  41 us (31%)
  Pallas kernels  35.3 us (27%)
  starting transfers between devices  27.5 us (21%)
  waiting for transfers between devices  19.8 us (15%)
  local copies, waits for them, and re-layouts  7.49 us (6%)
    all_to_all x3, blocking collectives, exchange(): return lax.all_to_all(x, axes, 0, 0)  41 us
    pallas_call x2, Pallas kernels, tiles(): pl.pallas_call(functools.partial(tiles_kernel, offsets, first), out_shape...  22.7 us
    all_to_all x2, waiting for transfers between devices, exchange(): return lax.all_to_all(x, axes, 0, 0)  19.8 us
    all_to_all x2, starting transfers between devices, exchange(): return lax.all_to_all(x, axes, 0, 0)  17.4 us
    pallas_call x1, Pallas kernels, factors(): pl.pallas_call(functools.partial(factor_kernel, scales), out_shape=(jax.S...  11.8 us
    ppermute x1, starting transfers between devices, body(): below = lax.ppermute(packed, leaf, up).reshape(BLOCKS, BOX, 128)  5.39 us
    unnamed x12, local copies, waits for them, and re-layouts  5.01 us
    ppermute x1, starting transfers between devices, body(): lax.ppermute(packed, leaf, [(b, a) for a, b in up])  4.72 us
  transfers between devices with their start and end apart: 4, of which 2 were waited for; matrix products, arithmetic and copies ran while one was open for 1% of the time, Pallas kernels for 8%

profile of v1, /device:TPU:1, one launch (start us, length us, event | category | flops | bytes accessed | tf_op | source)
XLA Modules:
  0.0 132.0 jit_solution(168916403143287968)
XLA Ops:
  0.6 0.0 copy-start.4
  0.6 1.0 constant_dynamic-update-slice_fusion.1
  1.7 0.0 copy-done.4
  1.7 5.4 %collective-permute-start = (bf16[2048,128]{0,1:T(8,128)(2,1)S(1)}, bf16[2048,128]{0,1:T(8,128)(2,1)S(1)}, u32[]{:S(2)}, u32[]{:S(2)}) collective-permute-start(bf16[2048,128]{0,1:T(8,128)(2,1)S(1)} %constant_dynamic-update-slice_fusion), channel_id=1, source_target_pairs={{0,4},{4,8},{8,12},{12,16},{16,20},{20,24},{24,28},{28,32},{32,36}... | collective-permute-start | bytes 1572872 | tf_op jit(solution)/shard_map/ppermute | solution.py:327
  7.1 4.7 %collective-permute-start.1 = (bf16[2048,128]{0,1:T(8,128)(2,1)S(1)}, bf16[2048,128]{0,1:T(8,128)(2,1)S(1)}, u32[]{:S(2)}, u32[]{:S(2)}) collective-permute-start(bf16[2048,128]{0,1:T(8,128)(2,1)S(1)} %constant_dynamic-update-slice_fusion), channel_id=1, source_target_pairs={{4,0},{8,4},{12,8},{16,12},{20,16},{24,20},{28,24},{32,28},{36,32}... | collective-permute-start | bytes 1572872 | tf_op jit(solution)/shard_map/ppermute | solution.py:328
  11.8 0.3 copy.11
  12.1 0.0 copy-start
  12.1 0.0 copy-start.1
  12.1 0.7 copy-done
  12.8 0.0 copy-done.1
  12.8 10.9 %shard_map.67.rest_2_ = f32[8,256,128]{2,1,0:T(8,128)S(1)} custom-call(s32[1]{0:T(128)} %bitcast.base_ref, s32[8,16]{1,0:T(8,128)S(1)} %copy-done, s32[8]{0:T(128)S(1)} %copy-done.1, bf16[8,256,128]{2,1,0:T(8,128)(2,1)S(1)} %bitcast.10, bf16[8,256,128]{2,1,0:T(8,128)(2,1)S(1)} %bitcast.11), custom_call_target="tpu_custom_call" | custom-call | flops 4026531840 | bytes 4194304 | tf_op jit(solution)/shard_map/pallas_call | solution.py:176
  23.7 0.0 copy-start.2
  23.7 1.0 copy-done.2
  24.7 0.0 collective-permute-done
  24.7 0.3 copy.12
  24.9 0.0 collective-permute-done.1
  24.9 0.3 copy.13
  25.2 0.0 copy-start.3
  25.2 1.2 copy-done.3
  26.5 11.9 %shard_map.68 = (f32[2048,64]{1,0:T(8,128)S(1)}, f32[4,256,128]{2,1,0:T(8,128)S(1)}) custom-call(s32[1]{0:T(128)} %bitcast.base_ref, s32[8,16]{1,0:T(8,128)S(1)} %copy-done, s32[8]{0:T(128)S(1)} %copy-done.1, bf16[8,256,128]{2,1,0:T(8,128)(2,1)S(1)} %bitcast.12, bf16[8,256,128]{2,1,0:T(8,128)(2,1)S(1)} %bitcast.13, bf16[8,256,128]{2,1,0:T(8,128)(2,1)S(1)} %bitcast.14, ...), custom_call_target="tpu_custom_call" | custom-call | flops 4026531840 | bytes 4194304 | tf_op jit(solution)/shard_map/pallas_call | solution.py:176
  38.3 11.0 %all_to_all.25.columns_ref = f32[4,256,128]{2,1,0:T(8,128)S(1)} all-to-all(f32[4,256,128]{2,1,0:T(8,128)S(1)} %get-tuple-element.8), channel_id=1, replica_groups=mesh['y'=8,'z'=8,'c'=2,'x'=4] {'x'}, dimensions={0} | all-to-all | bytes 1048576 | tf_op jit(solution)/shard_map/all_to_all | solution.py:314
  49.3 0.8 shard_map.69
  50.2 10.1 %all_to_all.26 = f32[8,48,128]{2,1,0:T(8,128)S(1)} all-to-all(f32[8,48,128]{2,1,0:T(8,128)S(1)} %bitcast.9), channel_id=1, replica_groups=mesh['y'=8,'z'=8,'c'=2,'x'=4] {'c','x'}, dimensions={0} | all-to-all | bytes 393216 | tf_op jit(solution)/shard_map/all_to_all | solution.py:314
  60.3 19.8 %all_to_all.27 = f32[8,48,128]{2,1,0:T(8,128)S(1)} all-to-all(f32[8,48,128]{2,1,0:T(8,128)S(1)} %broadcast_in_dim.6), channel_id=1, replica_groups=mesh['y'=8,'z'=8,'c'=2,'x'=4] {'z'}, dimensions={0} | all-to-all | bytes 393216 | tf_op jit(solution)/shard_map/all_to_all | solution.py:314
  80.2 0.7 broadcast_in_dim.7
  80.9 10.6 %all-to-all-start.3 = ((f32[8,48,128]{2,1,0:T(8,128)}), f32[8,48,128]{2,1,0:T(8,128)S(1)}, u32[]{:S(2)}, u32[]{:S(2)}) async-start(f32[8,48,128]{2,1,0:T(8,128)} %broadcast_in_dim.7), calls=%async_computation.3 | async-start | bytes 393216 | tf_op jit(solution)/shard_map/all_to_all | solution.py:314
  91.5 8.7 %all-to-all-done.3 = f32[8,48,128]{2,1,0:T(8,128)S(1)} async-done(((f32[8,48,128]{2,1,0:T(8,128)}), f32[8,48,128]{2,1,0:T(8,128)S(1)}, u32[]{:S(2)}, u32[]{:S(2)}) %all-to-all-start.3) | async-done | bytes 196640 | tf_op jit(solution)/shard_map/all_to_all | solution.py:314
  100.3 0.9 broadcast_in_dim.8
  101.2 6.8 %all-to-all-start.4 = ((f32[8,4,48,128]{3,2,1,0:T(8,128)}), f32[8,4,48,128]{3,2,1,0:T(8,128)S(1)}, u32[]{:S(2)}, u32[]{:S(2)}) async-start(f32[8,4,48,128]{3,2,1,0:T(8,128)} %broadcast_in_dim.8), calls=%async_computation.4 | async-start | bytes 1572864 | tf_op jit(solution)/shard_map/all_to_all | solution.py:314
  108.0 1.1 copy.14
  109.1 11.1 %all-to-all-done.4.slices_ref = f32[8,4,48,128]{3,2,1,0:T(8,128)S(1)} async-done(((f32[8,4,48,128]{3,2,1,0:T(8,128)}), f32[8,4,48,128]{3,2,1,0:T(8,128)S(1)}, u32[]{:S(2)}, u32[]{:S(2)}) %all-to-all-start.4) | async-done | bytes 786464 | tf_op jit(solution)/shard_map/all_to_all | solution.py:314
  120.2 11.8 %shard_map.70 = (f32[1,3,256,256]{3,2,1,0:T(8,128)}, f32[256,256]{1,0:T(8,128)}) custom-call(f32[8,4,48,128]{3,2,1,0:T(8,128)S(1)} %all-to-all-done.4.slices_ref), custom_call_target="tpu_custom_call" | custom-call | tf_op jit(solution)/shard_map/pallas_call | solution.py:300
  (8 shorter events, 0.1 us)
Async XLA Ops:
  0.6 1.0 copy-start.4
  1.7 23.0 %collective-permute-start = (bf16[2048,128]{0,1:T(8,128)(2,1)S(1)}, bf16[2048,128]{0,1:T(8,128)(2,1)S(1)}, u32[]{:S(2)}, u32[]{:S(2)}) collective-permute-start(bf16[2048,128]{0,1:T(8,128)(2,1)S(1)} %constant_dynamic-update-slice_fusion), channel_id=1, source_target_pairs={{0,4},{4,8},{8,12},{12,16},{16,20},{20,24},{24,28},{28,32},{32,36}... | collective-permute-start | bytes 1572872 | tf_op jit(solution)/shard_map/ppermute | solution.py:327
  7.1 17.9 %collective-permute-start.1 = (bf16[2048,128]{0,1:T(8,128)(2,1)S(1)}, bf16[2048,128]{0,1:T(8,128)(2,1)S(1)}, u32[]{:S(2)}, u32[]{:S(2)}) collective-permute-start(bf16[2048,128]{0,1:T(8,128)(2,1)S(1)} %constant_dynamic-update-slice_fusion), channel_id=1, source_target_pairs={{4,0},{8,4},{12,8},{16,12},{20,16},{24,20},{28,24},{32,28},{36,32}... | collective-permute-start | bytes 1572872 | tf_op jit(solution)/shard_map/ppermute | solution.py:328
  12.1 0.7 copy-start
  12.1 0.7 copy-start.1
  23.7 1.0 copy-start.2
  25.2 1.2 copy-start.3
  80.9 19.4 %all-to-all-start.3 = ((f32[8,48,128]{2,1,0:T(8,128)}), f32[8,48,128]{2,1,0:T(8,128)S(1)}, u32[]{:S(2)}, u32[]{:S(2)}) async-start(f32[8,48,128]{2,1,0:T(8,128)} %broadcast_in_dim.7), calls=%async_computation.3 | async-start | bytes 393216 | tf_op jit(solution)/shard_map/all_to_all | solution.py:314
  101.2 19.0 %all-to-all-start.4 = ((f32[8,4,48,128]{3,2,1,0:T(8,128)}), f32[8,4,48,128]{3,2,1,0:T(8,128)S(1)}, u32[]{:S(2)}, u32[]{:S(2)}) async-start(f32[8,4,48,128]{3,2,1,0:T(8,128)} %broadcast_in_dim.8), calls=%async_computation.4 | async-start | bytes 1572864 | tf_op jit(solution)/shard_map/all_to_all | solution.py:314

commit v2 on v1

v2 whole, which is shorter than its diff:
```python
import functools

import jax
import jax.numpy as jnp
from jax import lax
from jax.experimental import pallas as pl
from jax.experimental.pallas import tpu as pltpu
from jax.sharding import Mesh, PartitionSpec as P

LEVELS = 3
BLOCKS = 8
BOX = 256
SLOTS = 16
GROUP = 8
ENTRIES = BLOCKS * SLOTS + 3 * GROUP
BF = jnp.bfloat16
F = jnp.float32
NN = (((1,), (0,)), ((), ()))
NT = (((1,), (1,)), ((), ()))
TN = (((0,), (0,)), ((), ()))
LOG2E_OVER_32 = 1.4426950408889634 / 32.0
LIMIT = 20 << 20
VM = pl.BlockSpec(memory_space=pltpu.VMEM)
SM = pl.BlockSpec(memory_space=pltpu.SMEM)


def dot(a, b, dims):
    return lax.dot_general(a, b, dims, preferred_element_type=F)


def split3(x):
    h = x.astype(BF)
    r = x - h.astype(F)
    m = r.astype(BF)
    return h, m, (r - m.astype(F)).astype(BF)


def squared(box):
    wide = box[64:128].astype(F)
    sq = jnp.sum(wide * wide, axis=0, keepdims=True)
    h = sq.astype(BF).astype(F)
    m = (sq - h).astype(BF).astype(F)
    return h, m, sq - h - m, lax.broadcasted_iota(jnp.int32, (16, BOX), 0)


def extended(head, points):
    return jnp.concatenate([head.astype(BF), jnp.zeros((48, BOX), BF), points], axis=0)


def other_side(box):
    h, m, l, row = squared(box)
    head = jnp.where(row == 0, h, jnp.where(row == 1, m, jnp.where(row == 2, l, jnp.where(row < 6, 1.0, 0.0))))
    return extended(head, box[64:128]).T


def own_side(box):
    h, m, l, row = squared(box)
    head = jnp.where(row < 3, -1.0, jnp.where(row == 3, -h, jnp.where(row == 4, -m, jnp.where(row == 5, -l, 0.0))))
    return extended(head, (box[64:128].astype(F) * 2.0).astype(BF))


def build_lists(base, list_ref, count_ref, own, halo):
    def of_box(b, counts):
        def of_slot(s, counts):
            in_own, in_halo = counts
            j = list_ref[b, s] - base
            own[0, in_own] = b
            own[1, in_own] = j
            halo[0, in_halo] = b
            halo[1, in_halo] = jnp.where(j < 0, j + BLOCKS, j)
            inside = jnp.logical_and(j >= 0, j < BLOCKS).astype(jnp.int32)
            return in_own + inside, in_halo + 1 - inside

        return lax.fori_loop(0, count_ref[b], of_slot, counts)

    return lax.fori_loop(0, BLOCKS, of_box, (jnp.int32(GROUP), jnp.int32(GROUP)))


def run_list(end, ids, null, own, other, probes, cross, parts, total):
    for e in range(GROUP):
        ids[0, end + e] = 0
        ids[1, end + e] = null

    def step(t, _):
        at = [t * GROUP + k for k in range(GROUP)]
        for k in range(GROUP):
            cross[k] = dot(other[ids[1, at[k]]], own[ids[0, at[k]]], NN)
        for k in range(GROUP):
            tile = jnp.exp2(cross[k] * LOG2E_OVER_32)
            h = tile.astype(BF)
            parts[k, 0:BOX] = h
            parts[k, BOX:2 * BOX] = (tile - h.astype(F)).astype(BF)
        for k in range(GROUP):
            left = probes[ids[1, at[k]]]
            i = ids[0, at[k]]
            total[i] = total[i] + dot(jnp.concatenate([left, left], axis=1), parts[k], NN)
        return 0

    lax.fori_loop(1, (end + GROUP - 1) // GROUP, step, 0)


def own_kernel(base_ref, list_ref, count_ref, own_ref, total, sides, halo_ids, halo_end, other, probes, ids, cross, parts):
    end, halo_end[0] = build_lists(base_ref[0], list_ref, count_ref, ids, halo_ids)
    for b in range(BLOCKS):
        box = own_ref[:, BOX * b:BOX * b + BOX]
        other[b] = other_side(box)
        sides[b] = own_side(box)
        probes[b] = box[0:64]
    other[BLOCKS] = jnp.zeros((BOX, 128), BF)
    probes[BLOCKS] = jnp.zeros((64, BOX), BF)
    total[...] = jnp.zeros_like(total)
    run_list(end, ids, BLOCKS, sides, other, probes, cross, parts, total)


def halo_kernel(ids_ref, end_ref, below_ref, above_ref, sides, part, turned, send, other, probes, ids, cross, parts, total):
    end = end_ref[0]

    def keep(e, _):
        ids[0, e] = ids_ref[0, e]
        ids[1, e] = ids_ref[1, e]
        return 0

    lax.fori_loop(GROUP, end, keep, 0)
    for q, ref in enumerate((below_ref, above_ref)):
        for b in range(BLOCKS):
            box = ref[:, BOX * b:BOX * b + BOX]
            other[BLOCKS * q + b] = other_side(box)
            probes[BLOCKS * q + b] = box[0:64]
    other[2 * BLOCKS] = jnp.zeros((BOX, 128), BF)
    probes[2 * BLOCKS] = jnp.zeros((64, BOX), BF)
    total[...] = part[...]
    run_list(end, ids, 2 * BLOCKS, sides, other, probes, cross, parts, total)
    for b in range(BLOCKS):
        turned[:, BOX * b:BOX * b + BOX] = total[b]
        send[b // 2, b % 2] = total[b]


def list_scratch(boxes):
    return [
        pltpu.VMEM((boxes + 1, BOX, 128), BF),
        pltpu.VMEM((boxes + 1, 64, BOX), BF),
        pltpu.SMEM((2, ENTRIES), jnp.int32),
        pltpu.VMEM((GROUP, BOX, BOX), F),
        pltpu.VMEM((GROUP, 2 * BOX, BOX), BF),
    ]


def tiles_cost():
    return pl.CostEstimate(
        flops=64 * 3 * BOX * BOX * 128 * 2, bytes_accessed=4 << 20, transcendentals=64 * BOX * BOX
    )


def own_tiles(base, near_list, near_count, own):
    return pl.pallas_call(
        own_kernel,
        out_shape=(
            jax.ShapeDtypeStruct((BLOCKS, 64, BOX), F),
            jax.ShapeDtypeStruct((BLOCKS, 128, BOX), BF),
            jax.ShapeDtypeStruct((2, ENTRIES), jnp.int32),
            jax.ShapeDtypeStruct((1,), jnp.int32),
        ),
        in_specs=[SM, SM, SM, VM],
        out_specs=(VM, VM, SM, SM),
        scratch_shapes=list_scratch(BLOCKS),
        compiler_params=pltpu.CompilerParams(vmem_limit_bytes=LIMIT),
        cost_estimate=tiles_cost(),
    )(base, near_list, near_count, own)


def halo_tiles(ids, end, below, above, sides, part):
    return pl.pallas_call(
        halo_kernel,
        out_shape=(
            jax.ShapeDtypeStruct((64, BLOCKS * BOX), F),
            jax.ShapeDtypeStruct((BLOCKS // 2, 2, 64, BOX), F),
        ),
        in_specs=[SM, SM] + [VM] * 4,
        out_specs=(VM, VM),
        scratch_shapes=list_scratch(2 * BLOCKS) + [pltpu.VMEM((BLOCKS, 64, BOX), F)],
        compiler_params=pltpu.CompilerParams(vmem_limit_bytes=LIMIT),
        cost_estimate=tiles_cost(),
    )(ids, end, below, above, sides, part)


def gram_kernel(columns_ref, out_ref):
    g = None
    for b in range(2):
        h, m, l = split3(jnp.concatenate([columns_ref[q, b] for q in range(4)], axis=0))
        left = jnp.concatenate([h, h, m, h, m, l], axis=1)
        right = jnp.concatenate([h, m, h, l, m, h], axis=1)
        term = dot(left, right, NT)
        g = term if g is None else g + term
    out_ref[0:128, :] = g[0:128, 0:128]
    out_ref[128:256, :] = g[0:128, 128:256]
    out_ref[256:384, :] = g[128:256, 128:256]


def gram(columns):
    return pl.pallas_call(
        gram_kernel,
        out_shape=jax.ShapeDtypeStruct((384, 128), F),
        in_specs=[VM],
        out_specs=VM,
        compiler_params=pltpu.CompilerParams(vmem_limit_bytes=LIMIT),
    )(columns)


def panel_step(rows, off, width):
    n = len(rows)
    lanes = range(width // 128)
    sub = lax.broadcasted_iota(jnp.int32, (8, 128), 0)
    part = [[[r[8 * g:8 * g + 8, 128 * q:128 * q + 128] for q in lanes] for g in range(4)] for r in rows]
    for s in range(4):
        at = off + 8 * s
        cols = [
            [
                None if g < s else [
                    jnp.broadcast_to(part[b][g][0][:, at + j:at + j + 1], (8, 128)) for j in range(8)
                ]
                for g in range(4)
            ]
            for b in range(n)
        ]
        scale = [None] * n
        for j in range(8):
            for b in range(n):
                here = cols[b][s]
                pivot = jnp.broadcast_to(here[j][j:j + 1, :], (8, 128))
                inverse = 1.0 / pivot
                root = lax.rsqrt(pivot)
                scale[b] = root if j == 0 else jnp.where(sub == j, root, scale[b])
                ratio = [
                    None if l <= j else jnp.broadcast_to(here[l][j:j + 1, :], (8, 128)) * inverse
                    for l in range(8)
                ]
                row = [jnp.broadcast_to(part[b][s][q][j:j + 1, :], (8, 128)) * inverse for q in lanes]
                for g in range(s, 4):
                    c = cols[b][g][j]
                    for l in range(j + 1, 8):
                        cols[b][g][l] = cols[b][g][l] - c * ratio[l]
                    if g == s:
                        c = jnp.where(sub > j, c, 0.0)
                    part[b][g] = [part[b][g][q] - c * row[q] for q in lanes]
        for b in range(n):
            part[b][s] = [v * scale[b] for v in part[b][s]]
    return [jnp.concatenate([jnp.concatenate(v, axis=1) for v in p], axis=0) for p in part]


def factor(n, work, upper):
    for half in range(2):
        c0 = 128 * half
        for k in range(4):
            r0 = c0 + 32 * k
            rows = panel_step([work[b, r0:r0 + 32, c0:256] for b in range(n)], 32 * k, 256 - c0)
            for b in range(n):
                upper[b, r0:r0 + 32, c0:256] = rows[b]
            lo = r0 + 32
            if lo == 256:
                break
            for b in range(n):
                h, m, l = split3(rows[b])
                left = jnp.concatenate([h, h, m, h, m, l], axis=0)
                right = jnp.concatenate([h, m, h, l, m, h], axis=0)
                work[b, lo:256, c0:256] = work[b, lo:256, c0:256] - dot(left, right, TN)[lo - c0:, :]


def factor_kernel(scales, slices_ref, nodes_ref, root_ref, work, upper):
    n = len(scales)
    ri = lax.broadcasted_iota(jnp.int32, (128, 128), 0)
    ci = lax.broadcasted_iota(jnp.int32, (128, 128), 1)
    eye = jnp.where(ri == ci, 1.0, 0.0)
    for b in range(n):
        tri = jnp.concatenate([slices_ref[r, b] for r in range(8)], axis=0) * scales[b]
        work[b, 0:128, 0:128] = tri[0:128] + eye
        work[b, 0:128, 128:256] = tri[128:256]
        work[b, 128:256, 0:128] = jnp.zeros((128, 128), F)
        work[b, 128:256, 128:256] = tri[256:384] + eye
        upper[b, 128:256, 0:128] = jnp.zeros((128, 128), F)
    factor(n, work, upper)
    rows = lax.broadcasted_iota(jnp.int32, (256, 256), 0)
    cols = lax.broadcasted_iota(jnp.int32, (256, 256), 1)
    for b in range(n):
        low = jnp.where(rows >= cols, upper[b].T, 0.0)
        if b < LEVELS:
            nodes_ref[0, b] = low
        else:
            root_ref[...] = low


def factors(slices, scales):
    n = len(scales)
    return pl.pallas_call(
        functools.partial(factor_kernel, scales),
        out_shape=(
            jax.ShapeDtypeStruct((1, LEVELS, 256, 256), F),
            jax.ShapeDtypeStruct((256, 256), F),
        ),
        in_specs=[VM],
        out_specs=(VM, VM),
        scratch_shapes=[pltpu.VMEM((n, 256, 256), F)] * 2,
        compiler_params=pltpu.CompilerParams(vmem_limit_bytes=LIMIT),
    )(slices)


def exchange(x, axes):
    return lax.all_to_all(x, axes, 0, 0)


def to_all(x, axes, n):
    return exchange(jnp.broadcast_to(x[None], (n,) + x.shape), axes)


def body(points, probes, near_list, near_count):
    leaf = ("y", "z", "c")
    size = lax.axis_size(leaf)
    rows = points.shape[0]
    packed = jnp.concatenate([probes.T, points.T], axis=0)
    up = [(i, i + 1) for i in range(size - 1)]
    below = lax.ppermute(packed, leaf, up)
    above = lax.ppermute(packed, leaf, [(b, a) for a, b in up])
    base = (lax.axis_index(leaf) * BLOCKS).astype(jnp.int32).reshape(1)
    part, sides, ids, end = own_tiles(base, near_list, near_count, packed)
    turned, send = halo_tiles(ids, end, below, above, sides, part)
    samples = turned.T
    columns = exchange(send, "x")
    pieces = gram(columns).reshape(8, 48, 128)
    level1 = jnp.sum(exchange(pieces, ("c", "x")), axis=0)
    along_z = to_all(level1, "z", 8)
    z = lax.axis_index("z")
    pair = lax.dynamic_slice_in_dim(along_z, z // 2 * 2, 2, 0)
    four = lax.dynamic_slice_in_dim(along_z, z // 4 * 4, 4, 0)
    level2 = jnp.sum(pair, axis=0)
    level3 = jnp.sum(four, axis=0)
    along_y = to_all(jnp.sum(along_z, axis=0), "y", 8)
    root = jnp.sum(along_y, axis=0)
    slices = to_all(jnp.stack([level1, level2, level3, root]), ("c", "x"), 8)
    scales = [1.0 / (rows * 2 ** (l + 1)) for l in range(LEVELS)] + [1.0 / (rows * size)]
    node_factors, root_factor = factors(slices, scales)
    return samples, node_factors, root_factor


def solution(mesh):
    fine = Mesh(mesh.devices.reshape(8, 8, 2, 4), ("y", "z", "c", "x"))
    leaf = ("y", "z", "c")
    return jax.shard_map(
        body,
        mesh=fine,
        in_specs=(P(leaf, None), P(leaf, "x"), P(leaf, None), P(leaf)),
        out_specs=(P(leaf, "x"), P(leaf, None, None, None), P()),
        check_vma=False,
    )
```

time: 132 us -> 113 us (0.86)
  blocking collectives: 41 us -> 58 us
  waiting for transfers between devices: 19.8 us -> 8.73 us
  starting transfers between devices: 27.5 us -> 16.7 us
  Pallas kernels: 35.3 us -> 26.1 us
  local copies, waits for them, and re-layouts: 7.49 us -> 1.44 us
    all_to_all x3 -> x4, blocking collectives: 41 us -> 58 us  [exchange(): return lax.all_to_all(x, axes, 0, 0)]
    all_to_all x2 -> x1, waiting for transfers between devices: 19.8 us -> 8.72 us  [exchange(): return lax.all_to_all(x, axes, 0, 0)]
    all_to_all x2 -> x1, starting transfers between devices: 17.4 us -> 6.64 us  [exchange(): return lax.all_to_all(x, axes, 0, 0)]
    pallas_call x2, Pallas kernels: 22.7 us -> 13.7 us  [the longest x1 6.91 us: halo_tiles(): pl.pallas_call(halo_kernel, out_shape=(jax.ShapeDtypeStruct((64, BLOCKS *...]
    unnamed x12 -> x4, local copies, waits for them, and re-layouts: 5.01 us -> 0.67 us
  transfers between devices with their start and end apart: 4 -> 3, of which waited for: 2 -> 1; matrix products, arithmetic and copies ran while one was open for 1% -> 0% of each run, Pallas kernels for 8% -> 6%
where the time goes in v2:
time: 113 us
  blocking collectives  58 us (51%)
  Pallas kernels  26.1 us (23%)
  starting transfers between devices  16.7 us (15%)
  waiting for transfers between devices  8.73 us (8%)
  local copies, waits for them, and re-layouts  1.44 us (1%)
  other arithmetic  1.14 us (1%)
    all_to_all x4, blocking collectives, exchange(): return lax.all_to_all(x, axes, 0, 0)  58 us
    pallas_call x1, Pallas kernels, factors(): pl.pallas_call(functools.partial(factor_kernel, scales), out_shape=(jax.S...  11.8 us
    all_to_all x1, waiting for transfers between devices, exchange(): return lax.all_to_all(x, axes, 0, 0)  8.72 us
    pallas_call x1, Pallas kernels, halo_tiles(): pl.pallas_call(halo_kernel, out_shape=(jax.ShapeDtypeStruct((64, BLOCKS *...  6.91 us
    pallas_call x1, Pallas kernels, own_tiles(): pl.pallas_call(own_kernel, out_shape=(jax.ShapeDtypeStruct((BLOCKS, 64, B...  6.78 us
    all_to_all x1, starting transfers between devices, exchange(): return lax.all_to_all(x, axes, 0, 0)  6.64 us
    ppermute x1, starting transfers between devices, body(): below = lax.ppermute(packed, leaf, up)  5.39 us
    ppermute x1, starting transfers between devices, body(): above = lax.ppermute(packed, leaf, [(b, a) for a, b in up])  4.72 us
  transfers between devices with their start and end apart: 3, of which 1 were waited for; matrix products, arithmetic and copies ran while one was open for 0% of the time, Pallas kernels for 6%

profile of v2, /device:TPU:1, one launch (start us, length us, event | category | flops | bytes accessed | tf_op | source)
XLA Modules:
  0.0 112.9 jit_solution(16437377524889094232)
XLA Ops:
  0.6 1.1 pad_maximum_fusion.own_ref
  1.7 5.4 %collective-permute-start = (bf16[128,2048]{1,0:T(8,128)(2,1)S(1)}, bf16[128,2048]{1,0:T(8,128)(2,1)S(1)}, u32[]{:S(2)}, u32[]{:S(2)}) collective-permute-start(bf16[128,2048]{1,0:T(8,128)(2,1)S(1)} %pad_maximum_fusion.own_ref), channel_id=1, source_target_pairs={{0,4},{4,8},{8,12},{12,16},{16,20},{20,24},{24,28},{28,32},{32,36}... | collective-permute-start | bytes 1572872 | tf_op jit(solution)/shard_map/ppermute | solution.py:320
  7.1 4.7 %collective-permute-start.1 = (bf16[128,2048]{1,0:T(8,128)(2,1)S(1)}, bf16[128,2048]{1,0:T(8,128)(2,1)S(1)}, u32[]{:S(2)}, u32[]{:S(2)}) collective-permute-start(bf16[128,2048]{1,0:T(8,128)(2,1)S(1)} %pad_maximum_fusion.own_ref), channel_id=1, source_target_pairs={{4,0},{8,4},{12,8},{16,12},{20,16},{24,20},{28,24},{32,28},{36,32}... | collective-permute-start | bytes 1572872 | tf_op jit(solution)/shard_map/ppermute | solution.py:321
  11.8 0.0 copy-start
  11.8 0.0 copy-start.1
  11.9 0.7 copy-done
  12.5 0.0 copy-done.1
  12.5 6.8 %shard_map.67 = (f32[8,64,256]{2,1,0:T(8,128)S(1)}, bf16[8,128,256]{2,1,0:T(8,128)(2,1)S(1)}, s32[2,152]{1,0:T(2,128)S(1)}, s32[1]{0:T(128)}) custom-call(s32[1]{0:T(128)} %bitcast.base_ref, s32[8,16]{1,0:T(8,128)S(1)} %copy-done, s32[8]{0:T(128)S(1)} %copy-done.1, bf16[128,2048]{1,0:T(8,128)(2,1)S(1)} %pad_maximum_fusion.own_ref), custom_call_target="tpu_custom_call" | custom-call | flops 3221225472 | bytes 4194304 | tf_op jit(solution)/shard_map/pallas_call | solution.py:155
  19.3 0.0 collective-permute-done.below_ref
  19.3 0.0 collective-permute-done.1.above_ref
  19.3 6.9 %shard_map.68 = (f32[64,2048]{1,0:T(8,128)}, f32[4,2,64,256]{3,2,1,0:T(8,128)S(1)}) custom-call(s32[2,152]{1,0:T(2,128)S(1)} %get-tuple-element.11.ids_ref, s32[1]{0:T(128)} %get-tuple-element.12.end_ref, bf16[128,2048]{1,0:T(8,128)(2,1)S(1)} %collective-permute-done.below_ref, bf16[128,2048]{1,0:T(8,128)(2,1)S(1)} %collective-permute-done.1.above_ref, ...), custom_call_target="tpu_custom_call" | custom-call | flops 3221225472 | bytes 4194304 | tf_op jit(solution)/shard_map/pallas_call | solution.py:172
  26.2 9.4 %all_to_all.25.columns_ref = f32[4,2,64,256]{3,2,1,0:T(8,128)S(1)} all-to-all(f32[4,2,64,256]{3,2,1,0:T(8,128)S(1)} %get-tuple-element.16), channel_id=1, replica_groups=mesh['y'=8,'z'=8,'c'=2,'x'=4] {'x'}, dimensions={0} | all-to-all | bytes 1048576 | tf_op jit(solution)/shard_map/all_to_all | solution.py:307
  35.7 0.6 shard_map.69
  36.3 11.7 %all_to_all.26 = f32[8,48,128]{2,1,0:T(8,128)S(1)} all-to-all(f32[8,48,128]{2,1,0:T(8,128)S(1)} %bitcast.9), channel_id=1, replica_groups=mesh['y'=8,'z'=8,'c'=2,'x'=4] {'c','x'}, dimensions={0} | all-to-all | bytes 393216 | tf_op jit(solution)/shard_map/all_to_all | solution.py:307
  48.0 19.0 %all_to_all.27 = f32[8,48,128]{2,1,0:T(8,128)S(1)} all-to-all(f32[8,48,128]{2,1,0:T(8,128)S(1)} %broadcast_in_dim.6), channel_id=1, replica_groups=mesh['y'=8,'z'=8,'c'=2,'x'=4] {'z'}, dimensions={0} | all-to-all | bytes 393216 | tf_op jit(solution)/shard_map/all_to_all | solution.py:307
  67.0 0.7 broadcast_in_dim.7
  67.7 6.6 %all-to-all-start.3 = ((f32[8,48,128]{2,1,0:T(8,128)}), f32[8,48,128]{2,1,0:T(8,128)S(1)}, u32[]{:S(2)}, u32[]{:S(2)}) async-start(f32[8,48,128]{2,1,0:T(8,128)} %broadcast_in_dim.7), calls=%async_computation.3 | async-start | bytes 393216 | tf_op jit(solution)/shard_map/all_to_all | solution.py:307
  74.3 8.7 %all-to-all-done.3 = f32[8,48,128]{2,1,0:T(8,128)S(1)} async-done(((f32[8,48,128]{2,1,0:T(8,128)}), f32[8,48,128]{2,1,0:T(8,128)S(1)}, u32[]{:S(2)}, u32[]{:S(2)}) %all-to-all-start.3) | async-done | bytes 196640 | tf_op jit(solution)/shard_map/all_to_all | solution.py:307
  83.1 0.1 broadcast_in_dim.8
  83.2 17.9 %all_to_all.28.slices_ref = f32[8,4,48,128]{3,2,1,0:T(8,128)S(1)} all-to-all(f32[8,4,48,128]{3,2,1,0:T(8,128)S(1)} %broadcast_in_dim.8), channel_id=1, replica_groups=mesh['y'=8,'z'=8,'c'=2,'x'=4] {'c','x'}, dimensions={0} | all-to-all | bytes 1572864 | tf_op jit(solution)/shard_map/all_to_all | solution.py:307
  101.1 11.8 %shard_map.70 = (f32[1,3,256,256]{3,2,1,0:T(8,128)}, f32[256,256]{1,0:T(8,128)}) custom-call(f32[8,4,48,128]{3,2,1,0:T(8,128)S(1)} %all_to_all.28.slices_ref), custom_call_target="tpu_custom_call" | custom-call | tf_op jit(solution)/shard_map/pallas_call | solution.py:293
  (7 shorter events, 0.1 us)
Async XLA Ops:
  1.7 17.6 %collective-permute-start = (bf16[128,2048]{1,0:T(8,128)(2,1)S(1)}, bf16[128,2048]{1,0:T(8,128)(2,1)S(1)}, u32[]{:S(2)}, u32[]{:S(2)}) collective-permute-start(bf16[128,2048]{1,0:T(8,128)(2,1)S(1)} %pad_maximum_fusion.own_ref), channel_id=1, source_target_pairs={{0,4},{4,8},{8,12},{12,16},{16,20},{20,24},{24,28},{28,32},{32,36}... | collective-permute-start | bytes 1572872 | tf_op jit(solution)/shard_map/ppermute | solution.py:320
  7.1 12.2 %collective-permute-start.1 = (bf16[128,2048]{1,0:T(8,128)(2,1)S(1)}, bf16[128,2048]{1,0:T(8,128)(2,1)S(1)}, u32[]{:S(2)}, u32[]{:S(2)}) collective-permute-start(bf16[128,2048]{1,0:T(8,128)(2,1)S(1)} %pad_maximum_fusion.own_ref), channel_id=1, source_target_pairs={{4,0},{8,4},{12,8},{16,12},{20,16},{24,20},{28,24},{32,28},{36,32}... | collective-permute-start | bytes 1572872 | tf_op jit(solution)/shard_map/ppermute | solution.py:321
  11.8 0.7 copy-start
  11.8 0.7 copy-start.1
  67.7 15.4 %all-to-all-start.3 = ((f32[8,48,128]{2,1,0:T(8,128)}), f32[8,48,128]{2,1,0:T(8,128)S(1)}, u32[]{:S(2)}, u32[]{:S(2)}) async-start(f32[8,48,128]{2,1,0:T(8,128)} %broadcast_in_dim.7), calls=%async_computation.3 | async-start | bytes 393216 | tf_op jit(solution)/shard_map/all_to_all | solution.py:307

commit v3 on v2

--- a/solution.py
+++ b/solution.py
@@ -76,11 +76,7 @@
     return lax.fori_loop(0, BLOCKS, of_box, (jnp.int32(GROUP), jnp.int32(GROUP)))
 
 
-def run_list(end, ids, null, own, other, probes, cross, parts, total):
-    for e in range(GROUP):
-        ids[0, end + e] = 0
-        ids[1, end + e] = null
-
+def run_list(end, ids, own, other, probes, cross, parts, total):
     def step(t, _):
         at = [t * GROUP + k for k in range(GROUP)]
         for k in range(GROUP):
@@ -99,8 +95,16 @@
     lax.fori_loop(1, (end + GROUP - 1) // GROUP, step, 0)
 
 
-def own_kernel(base_ref, list_ref, count_ref, own_ref, total, sides, halo_ids, halo_end, other, probes, ids, cross, parts):
-    end, halo_end[0] = build_lists(base_ref[0], list_ref, count_ref, ids, halo_ids)
+def own_kernel(
+    base_ref, list_hbm, count_hbm, own_ref, total, sides, halo_ids, halo_end,
+    other, probes, cross, parts, ids, list_ref, count_ref, sems,
+):
+    copies = [
+        pltpu.make_async_copy(list_hbm, list_ref, sems.at[0]),
+        pltpu.make_async_copy(count_hbm, count_ref, sems.at[1]),
+    ]
+    for copy in copies:
+        copy.start()
     for b in range(BLOCKS):
         box = own_ref[:, BOX * b:BOX * b + BOX]
         other[b] = other_side(box)
@@ -109,18 +113,19 @@
     other[BLOCKS] = jnp.zeros((BOX, 128), BF)
     probes[BLOCKS] = jnp.zeros((64, BOX), BF)
     total[...] = jnp.zeros_like(total)
-    run_list(end, ids, BLOCKS, sides, other, probes, cross, parts, total)
-
-
-def halo_kernel(ids_ref, end_ref, below_ref, above_ref, sides, part, turned, send, other, probes, ids, cross, parts, total):
-    end = end_ref[0]
-
-    def keep(e, _):
-        ids[0, e] = ids_ref[0, e]
-        ids[1, e] = ids_ref[1, e]
-        return 0
-
-    lax.fori_loop(GROUP, end, keep, 0)
+    for copy in copies:
+        copy.wait()
+    end, end_halo = build_lists(base_ref[0], list_ref, count_ref, ids, halo_ids)
+    halo_end[0] = end_halo
+    for k in range(GROUP):
+        ids[0, end + k] = 0
+        ids[1, end + k] = BLOCKS
+        halo_ids[0, end_halo + k] = 0
+        halo_ids[1, end_halo + k] = 2 * BLOCKS
+    run_list(end, ids, sides, other, probes, cross, parts, total)
+
+
+def halo_kernel(ids, end_ref, below_ref, above_ref, sides, part, turned, send, other, probes, cross, parts, total):
     for q, ref in enumerate((below_ref, above_ref)):
         for b in range(BLOCKS):
             box = ref[:, BOX * b:BOX * b + BOX]
@@ -129,7 +134,7 @@
     other[2 * BLOCKS] = jnp.zeros((BOX, 128), BF)
     probes[2 * BLOCKS] = jnp.zeros((64, BOX), BF)
     total[...] = part[...]
-    run_list(end, ids, 2 * BLOCKS, sides, other, probes, cross, parts, total)
+    run_list(end_ref[0], ids, sides, other, probes, cross, parts, total)
     for b in range(BLOCKS):
         turned[:, BOX * b:BOX * b + BOX] = total[b]
         send[b // 2, b % 2] = total[b]
@@ -139,7 +144,6 @@
     return [
         pltpu.VMEM((boxes + 1, BOX, 128), BF),
         pltpu.VMEM((boxes + 1, 64, BOX), BF),
-        pltpu.SMEM((2, ENTRIES), jnp.int32),
         pltpu.VMEM((GROUP, BOX, BOX), F),
         pltpu.VMEM((GROUP, 2 * BOX, BOX), BF),
     ]
@@ -160,9 +164,15 @@
             jax.ShapeDtypeStruct((2, ENTRIES), jnp.int32),
             jax.ShapeDtypeStruct((1,), jnp.int32),
         ),
-        in_specs=[SM, SM, SM, VM],
+        in_specs=[SM, pl.BlockSpec(memory_space=pltpu.HBM), pl.BlockSpec(memory_space=pltpu.HBM), VM],
         out_specs=(VM, VM, SM, SM),
-        scratch_shapes=list_scratch(BLOCKS),
+        scratch_shapes=list_scratch(BLOCKS)
+        + [
+            pltpu.SMEM((2, ENTRIES), jnp.int32),
+            pltpu.SMEM((BLOCKS, SLOTS), jnp.int32),
+            pltpu.SMEM((BLOCKS,), jnp.int32),
+            pltpu.SemaphoreType.DMA((2,)),
+        ],
         compiler_params=pltpu.CompilerParams(vmem_limit_bytes=LIMIT),
         cost_estimate=tiles_cost(),
     )(base, near_list, near_count, own)
@@ -191,19 +201,34 @@
         right = jnp.concatenate([h, m, h, l, m, h], axis=1)
         term = dot(left, right, NT)
         g = term if g is None else g + term
-    out_ref[0:128, :] = g[0:128, 0:128]
-    out_ref[128:256, :] = g[0:128, 128:256]
-    out_ref[256:384, :] = g[128:256, 128:256]
+    out_ref[0:64, :] = g[0:64, 0:128]
+    out_ref[64:128, :] = g[0:64, 128:256]
+    out_ref[128:192, :] = g[64:128, 128:256]
+    out_ref[192:256, :] = g[128:192, 128:256]
+    low_lanes = lax.broadcasted_iota(jnp.int32, (64, 128), 1) < 64
+    out_ref[256:320, :] = jnp.where(low_lanes, pltpu.roll(g[192:256, 128:256], 64, 1), g[64:128, 0:128])
 
 
 def gram(columns):
     return pl.pallas_call(
         gram_kernel,
-        out_shape=jax.ShapeDtypeStruct((384, 128), F),
+        out_shape=jax.ShapeDtypeStruct((320, 128), F),
         in_specs=[VM],
         out_specs=VM,
         compiler_params=pltpu.CompilerParams(vmem_limit_bytes=LIMIT),
     )(columns)
+
+
+def lane_of(x, lane):
+    index = jnp.full((8, 128, 1), lane, jnp.int32)
+    dims = lax.GatherDimensionNumbers(
+        offset_dims=(),
+        collapsed_slice_dims=(1,),
+        start_index_map=(1,),
+        operand_batching_dims=(0,),
+        start_indices_batching_dims=(0,),
+    )
+    return lax.gather(x, index, dims, (1, 1), mode=lax.GatherScatterMode.PROMISE_IN_BOUNDS)
 
 
 def panel_step(rows, off, width):
@@ -214,28 +239,26 @@
     for s in range(4):
         at = off + 8 * s
         cols = [
-            [
-                None if g < s else [
-                    jnp.broadcast_to(part[b][g][0][:, at + j:at + j + 1], (8, 128)) for j in range(8)
-                ]
-                for g in range(4)
-            ]
+            [None if g < s else [lane_of(part[b][g][0], at + j) for j in range(8)] for g in range(4)]
             for b in range(n)
         ]
-        scale = [None] * n
+        pivots = [None] * n
         for j in range(8):
             for b in range(n):
                 here = cols[b][s]
                 pivot = jnp.broadcast_to(here[j][j:j + 1, :], (8, 128))
                 inverse = 1.0 / pivot
-                root = lax.rsqrt(pivot)
-                scale[b] = root if j == 0 else jnp.where(sub == j, root, scale[b])
+                pivots[b] = pivot if j == 0 else jnp.where(sub == j, pivot, pivots[b])
+                if j == 7 and s == 3:
+                    continue
                 ratio = [
                     None if l <= j else jnp.broadcast_to(here[l][j:j + 1, :], (8, 128)) * inverse
                     for l in range(8)
                 ]
                 row = [jnp.broadcast_to(part[b][s][q][j:j + 1, :], (8, 128)) * inverse for q in lanes]
                 for g in range(s, 4):
+                    if g == s and j == 7:
+                        continue
                     c = cols[b][g][j]
                     for l in range(j + 1, 8):
                         cols[b][g][l] = cols[b][g][l] - c * ratio[l]
@@ -243,7 +266,8 @@
                         c = jnp.where(sub > j, c, 0.0)
                     part[b][g] = [part[b][g][q] - c * row[q] for q in lanes]
         for b in range(n):
-            part[b][s] = [v * scale[b] for v in part[b][s]]
+            scale = lax.rsqrt(pivots[b])
+            part[b][s] = [v * scale for v in part[b][s]]
     return [jnp.concatenate([jnp.concatenate(v, axis=1) for v in p], axis=0) for p in part]
 
 
@@ -262,7 +286,13 @@
                 h, m, l = split3(rows[b])
                 left = jnp.concatenate([h, h, m, h, m, l], axis=0)
                 right = jnp.concatenate([h, m, h, l, m, h], axis=0)
-                work[b, lo:256, c0:256] = work[b, lo:256, c0:256] - dot(left, right, TN)[lo - c0:, :]
+                update = dot(left, right, TN)
+                if half == 0:
+                    if lo < 128:
+                        work[b, lo:128, :] = work[b, lo:128, :] - update[lo:128, :]
+                    work[b, 128:256, 128:256] = work[b, 128:256, 128:256] - update[128:256, 128:256]
+                else:
+                    work[b, lo:256, 128:256] = work[b, lo:256, 128:256] - update[lo - 128:128, :]
 
 
 def factor_kernel(scales, slices_ref, nodes_ref, root_ref, work, upper):
@@ -271,17 +301,26 @@
     ci = lax.broadcasted_iota(jnp.int32, (128, 128), 1)
     eye = jnp.where(ri == ci, 1.0, 0.0)
     for b in range(n):
-        tri = jnp.concatenate([slices_ref[r, b] for r in range(8)], axis=0) * scales[b]
-        work[b, 0:128, 0:128] = tri[0:128] + eye
-        work[b, 0:128, 128:256] = tri[128:256]
-        work[b, 128:256, 0:128] = jnp.zeros((128, 128), F)
-        work[b, 128:256, 128:256] = tri[256:384] + eye
-        upper[b, 128:256, 0:128] = jnp.zeros((128, 128), F)
+        t = jnp.concatenate([slices_ref[r, b] for r in range(8)], axis=0) * scales[b]
+        work[b, 0:64, 0:128] = t[0:64] + eye[0:64]
+        work[b, 0:64, 128:256] = t[64:128]
+        work[b, 64:128, 0:128] = t[256:320] + eye[64:128]
+        work[b, 64:128, 128:256] = t[128:192]
+        work[b, 128:192, 128:256] = t[192:256] + eye[0:64]
+        work[b, 192:256, 128:256] = pltpu.roll(t[256:320], 64, 1) + eye[64:128]
     factor(n, work, upper)
-    rows = lax.broadcasted_iota(jnp.int32, (256, 256), 0)
-    cols = lax.broadcasted_iota(jnp.int32, (256, 256), 1)
+    below = ri >= ci
     for b in range(n):
-        low = jnp.where(rows >= cols, upper[b].T, 0.0)
+        first = jnp.where(below, upper[b, 0:128, 0:128].T, 0.0)
+        cross = upper[b, 0:128, 128:256].T
+        second = jnp.where(below, upper[b, 128:256, 128:256].T, 0.0)
+        low = jnp.concatenate(
+            [
+                jnp.concatenate([first, jnp.zeros((128, 128), F)], axis=1),
+                jnp.concatenate([cross, second], axis=1),
+            ],
+            axis=0,
+        )
         if b < LEVELS:
             nodes_ref[0, b] = low
         else:
@@ -324,7 +363,7 @@
     turned, send = halo_tiles(ids, end, below, above, sides, part)
     samples = turned.T
     columns = exchange(send, "x")
-    pieces = gram(columns).reshape(8, 48, 128)
+    pieces = gram(columns).reshape(8, 40, 128)
     level1 = jnp.sum(exchange(pieces, ("c", "x")), axis=0)
     along_z = to_all(level1, "z", 8)
     z = lax.axis_index("z")
@@ -332,7 +371,9 @@
     four = lax.dynamic_slice_in_dim(along_z, z // 4 * 4, 4, 0)
     level2 = jnp.sum(pair, axis=0)
     level3 = jnp.sum(four, axis=0)
-    along_y = to_all(jnp.sum(along_z, axis=0), "y", 8)
+    line = jnp.sum(along_z, axis=0)
+    level2, level3, line = lax.optimization_barrier((level2, level3, line))
+    along_y = to_all(line, "y", 8)
     root = jnp.sum(along_y, axis=0)
     slices = to_all(jnp.stack([level1, level2, level3, root]), ("c", "x"), 8)
     scales = [1.0 / (rows * 2 ** (l + 1)) for l in range(LEVELS)] + [1.0 / (rows * size)]

time: 113 us -> 108 us (0.956)
  blocking collectives: 58 us -> 49.8 us
  starting transfers between devices: 16.7 us -> 22.7 us
  Pallas kernels: 26.1 us -> 23.5 us
    all_to_all x4, blocking collectives: 58 us -> 49.8 us  [exchange(): return lax.all_to_all(x, axes, 0, 0)]
    all_to_all x1, starting transfers between devices: 6.64 us -> 12.6 us  [exchange(): return lax.all_to_all(x, axes, 0, 0)]
    pallas_call x1, Pallas kernels: 11.8 us -> 9.54 us  [factors(): pl.pallas_call(functools.partial(factor_kernel, scales), out_shape=(jax.S...]
where the time goes in v3:
time: 108 us
  blocking collectives  49.8 us (46%)
  Pallas kernels  23.5 us (22%)
  starting transfers between devices  22.7 us (21%)
  waiting for transfers between devices  8.63 us (8%)
  local copies, waits for them, and re-layouts  1.41 us (1%)
  other arithmetic  1.15 us (1%)
    all_to_all x4, blocking collectives, exchange(): return lax.all_to_all(x, axes, 0, 0)  49.8 us
    all_to_all x1, starting transfers between devices, exchange(): return lax.all_to_all(x, axes, 0, 0)  12.6 us
    pallas_call x1, Pallas kernels, factors(): pl.pallas_call(functools.partial(factor_kernel, scales), out_shape=(jax.S...  9.54 us
    all_to_all x1, waiting for transfers between devices, exchange(): return lax.all_to_all(x, axes, 0, 0)  8.62 us
    pallas_call x1, Pallas kernels, own_tiles(): pl.pallas_call(own_kernel, out_shape=(jax.ShapeDtypeStruct((BLOCKS, 64, B...  6.64 us
    pallas_call x1, Pallas kernels, halo_tiles(): pl.pallas_call(halo_kernel, out_shape=(jax.ShapeDtypeStruct((64, BLOCKS *...  6.62 us
    ppermute x1, starting transfers between devices, body(): below = lax.ppermute(packed, leaf, up)  5.39 us
    ppermute x1, starting transfers between devices, body(): above = lax.ppermute(packed, leaf, [(b, a) for a, b in up])  4.72 us
  transfers between devices with their start and end apart: 3, of which 1 were waited for; matrix products, arithmetic and copies ran while one was open for 0% of the time, Pallas kernels for 6%

profile of v3, /device:TPU:1, one launch (start us, length us, event | category | flops | bytes accessed | tf_op | source)
XLA Modules:
  0.0 107.9 jit_solution(13580265317563511949)
XLA Ops:
  0.6 1.1 pad_maximum_fusion.own_ref
  1.7 5.4 %collective-permute-start = (bf16[128,2048]{1,0:T(8,128)(2,1)S(1)}, bf16[128,2048]{1,0:T(8,128)(2,1)S(1)}, u32[]{:S(2)}, u32[]{:S(2)}) collective-permute-start(bf16[128,2048]{1,0:T(8,128)(2,1)S(1)} %pad_maximum_fusion.own_ref), channel_id=1, source_target_pairs={{0,4},{4,8},{8,12},{12,16},{16,20},{20,24},{24,28},{28,32},{32,36}... | collective-permute-start | bytes 1572872 | tf_op jit(solution)/shard_map/ppermute | solution.py:359
  7.1 4.7 %collective-permute-start.1 = (bf16[128,2048]{1,0:T(8,128)(2,1)S(1)}, bf16[128,2048]{1,0:T(8,128)(2,1)S(1)}, u32[]{:S(2)}, u32[]{:S(2)}) collective-permute-start(bf16[128,2048]{1,0:T(8,128)(2,1)S(1)} %pad_maximum_fusion.own_ref), channel_id=1, source_target_pairs={{4,0},{8,4},{12,8},{16,12},{20,16},{24,20},{28,24},{32,28},{36,32}... | collective-permute-start | bytes 1572872 | tf_op jit(solution)/shard_map/ppermute | solution.py:360
  11.8 0.0 copy-start
  11.8 0.0 copy-start.1
  11.9 0.7 copy-done
  12.5 0.0 copy-done.1
  12.5 6.6 %shard_map.67 = (f32[8,64,256]{2,1,0:T(8,128)S(1)}, bf16[8,128,256]{2,1,0:T(8,128)(2,1)S(1)}, s32[2,152]{1,0:T(2,128)S(1)}, s32[1]{0:T(128)}) custom-call(s32[1]{0:T(128)} %bitcast.base_ref, s32[8,16]{1,0:T(8,128)S(1)} %copy-done, s32[8]{0:T(128)S(1)} %copy-done.1, bf16[128,2048]{1,0:T(8,128)(2,1)S(1)} %pad_maximum_fusion.own_ref), custom_call_target="tpu_custom_call" | custom-call | flops 3221225472 | bytes 4194304 | tf_op jit(solution)/shard_map/pallas_call | solution.py:159
  19.2 0.0 collective-permute-done.below_ref
  19.2 0.0 collective-permute-done.1.above_ref
  19.2 6.6 %shard_map.68 = (f32[64,2048]{1,0:T(8,128)}, f32[4,2,64,256]{3,2,1,0:T(8,128)S(1)}) custom-call(s32[2,152]{1,0:T(2,128)S(1)} %get-tuple-element.14.ids, s32[1]{0:T(128)} %get-tuple-element.15.end_ref, bf16[128,2048]{1,0:T(8,128)(2,1)S(1)} %collective-permute-done.below_ref, bf16[128,2048]{1,0:T(8,128)(2,1)S(1)} %collective-permute-done.1.above_ref, ...), custom_call_target="tpu_custom_call" | custom-call | flops 3221225472 | bytes 4194304 | tf_op jit(solution)/shard_map/pallas_call | solution.py:182
  25.8 9.3 %all_to_all.25.columns_ref = f32[4,2,64,256]{3,2,1,0:T(8,128)S(1)} all-to-all(f32[4,2,64,256]{3,2,1,0:T(8,128)S(1)} %get-tuple-element.19), channel_id=1, replica_groups=mesh['y'=8,'z'=8,'c'=2,'x'=4] {'x'}, dimensions={0} | all-to-all | bytes 1048576 | tf_op jit(solution)/shard_map/all_to_all | solution.py:346
  35.1 0.7 shard_map.69
  35.8 7.9 %all_to_all.26 = f32[8,40,128]{2,1,0:T(8,128)S(1)} all-to-all(f32[8,40,128]{2,1,0:T(8,128)S(1)} %bitcast.9), channel_id=1, replica_groups=mesh['y'=8,'z'=8,'c'=2,'x'=4] {'c','x'}, dimensions={0} | all-to-all | bytes 327680 | tf_op jit(solution)/shard_map/all_to_all | solution.py:346
  43.7 0.7 broadcast_in_dim.6
  44.4 12.6 %all-to-all-start.2 = ((f32[8,40,128]{2,1,0:T(8,128)}), f32[8,40,128]{2,1,0:T(8,128)S(1)}, u32[]{:S(2)}, u32[]{:S(2)}) async-start(f32[8,40,128]{2,1,0:T(8,128)} %broadcast_in_dim.6), calls=%async_computation.2 | async-start | bytes 327680 | tf_op jit(solution)/shard_map/all_to_all | solution.py:346
  56.9 8.6 %all-to-all-done.2 = f32[8,40,128]{2,1,0:T(8,128)S(1)} async-done(((f32[8,40,128]{2,1,0:T(8,128)}), f32[8,40,128]{2,1,0:T(8,128)S(1)}, u32[]{:S(2)}, u32[]{:S(2)}) %all-to-all-start.2) | async-done | bytes 163872 | tf_op jit(solution)/shard_map/all_to_all | solution.py:346
  65.6 16.0 %all_to_all.27 = f32[8,40,128]{2,1,0:T(8,128)S(1)} all-to-all(f32[8,40,128]{2,1,0:T(8,128)S(1)} %broadcast_in_dim.7), channel_id=1, replica_groups=mesh['y'=8,'z'=8,'c'=2,'x'=4] {'y'}, dimensions={0} | all-to-all | bytes 327680 | tf_op jit(solution)/shard_map/all_to_all | solution.py:346
  81.8 16.6 %all_to_all.28.slices_ref = f32[8,4,40,128]{3,2,1,0:T(8,128)S(1)} all-to-all(f32[8,4,40,128]{3,2,1,0:T(8,128)S(1)} %broadcast_in_dim.8), channel_id=1, replica_groups=mesh['y'=8,'z'=8,'c'=2,'x'=4] {'c','x'}, dimensions={0} | all-to-all | bytes 1310720 | tf_op jit(solution)/shard_map/all_to_all | solution.py:346
  98.4 9.5 %shard_map.70 = (f32[1,3,256,256]{3,2,1,0:T(8,128)}, f32[256,256]{1,0:T(8,128)}) custom-call(f32[8,4,40,128]{3,2,1,0:T(8,128)S(1)} %all_to_all.28.slices_ref), custom_call_target="tpu_custom_call" | custom-call | tf_op jit(solution)/shard_map/pallas_call | solution.py:332
  (8 shorter events, 0.1 us)
Async XLA Ops:
  1.7 17.5 %collective-permute-start = (bf16[128,2048]{1,0:T(8,128)(2,1)S(1)}, bf16[128,2048]{1,0:T(8,128)(2,1)S(1)}, u32[]{:S(2)}, u32[]{:S(2)}) collective-permute-start(bf16[128,2048]{1,0:T(8,128)(2,1)S(1)} %pad_maximum_fusion.own_ref), channel_id=1, source_target_pairs={{0,4},{4,8},{8,12},{12,16},{16,20},{20,24},{24,28},{28,32},{32,36}... | collective-permute-start | bytes 1572872 | tf_op jit(solution)/shard_map/ppermute | solution.py:359
  7.1 12.1 %collective-permute-start.1 = (bf16[128,2048]{1,0:T(8,128)(2,1)S(1)}, bf16[128,2048]{1,0:T(8,128)(2,1)S(1)}, u32[]{:S(2)}, u32[]{:S(2)}) collective-permute-start(bf16[128,2048]{1,0:T(8,128)(2,1)S(1)} %pad_maximum_fusion.own_ref), channel_id=1, source_target_pairs={{4,0},{8,4},{12,8},{16,12},{20,16},{24,20},{28,24},{32,28},{36,32}... | collective-permute-start | bytes 1572872 | tf_op jit(solution)/shard_map/ppermute | solution.py:360
  11.8 0.7 copy-start
  11.8 0.7 copy-start.1
  44.4 21.2 %all-to-all-start.2 = ((f32[8,40,128]{2,1,0:T(8,128)}), f32[8,40,128]{2,1,0:T(8,128)S(1)}, u32[]{:S(2)}, u32[]{:S(2)}) async-start(f32[8,40,128]{2,1,0:T(8,128)} %broadcast_in_dim.6), calls=%async_computation.2 | async-start | bytes 327680 | tf_op jit(solution)/shard_map/all_to_all | solution.py:346

commit v4 on v3

--- a/solution.py
+++ b/solution.py
@@ -60,6 +60,8 @@
 
 
 def build_lists(base, list_ref, count_ref, own, halo):
+    core = (base // BLOCKS) % 2
+
     def of_box(b, counts):
         def of_slot(s, counts):
             in_own, in_halo = counts
@@ -67,7 +69,8 @@
             own[0, in_own] = b
             own[1, in_own] = j
             halo[0, in_halo] = b
-            halo[1, in_halo] = jnp.where(j < 0, j + BLOCKS, j)
+            before = (j < 0).astype(jnp.int32)
+            halo[1, in_halo] = jnp.where(j < 0, j + BLOCKS, j - BLOCKS) + BLOCKS * (before ^ core)
             inside = jnp.logical_and(j >= 0, j < BLOCKS).astype(jnp.int32)
             return in_own + inside, in_halo + 1 - inside
 
@@ -125,8 +128,8 @@
     run_list(end, ids, sides, other, probes, cross, parts, total)
 
 
-def halo_kernel(ids, end_ref, below_ref, above_ref, sides, part, turned, send, other, probes, cross, parts, total):
-    for q, ref in enumerate((below_ref, above_ref)):
+def halo_kernel(ids, end_ref, near_ref, far_ref, sides, part, turned, send, other, probes, cross, parts, total):
+    for q, ref in enumerate((near_ref, far_ref)):
         for b in range(BLOCKS):
             box = ref[:, BOX * b:BOX * b + BOX]
             other[BLOCKS * q + b] = other_side(box)
@@ -178,7 +181,7 @@
     )(base, near_list, near_count, own)
 
 
-def halo_tiles(ids, end, below, above, sides, part):
+def halo_tiles(ids, end, near, far, sides, part):
     return pl.pallas_call(
         halo_kernel,
         out_shape=(
@@ -190,7 +193,7 @@
         scratch_shapes=list_scratch(2 * BLOCKS) + [pltpu.VMEM((BLOCKS, 64, BOX), F)],
         compiler_params=pltpu.CompilerParams(vmem_limit_bytes=LIMIT),
         cost_estimate=tiles_cost(),
-    )(ids, end, below, above, sides, part)
+    )(ids, end, near, far, sides, part)
 
 
 def gram_kernel(columns_ref, out_ref):
@@ -342,6 +345,30 @@
     )(slices)
 
 
+def line_kernel(base_ref, slices, level2, level3, line):
+    z = base_ref[0] // (2 * BLOCKS) % 8
+    two = z // 2 * 2
+    four = z // 4 * 4
+    level2[...] = slices[two] + slices[two + 1]
+    level3[...] = (slices[four] + slices[four + 1]) + (slices[four + 2] + slices[four + 3])
+    low = (slices[0] + slices[1]) + (slices[2] + slices[3])
+    high = (slices[4] + slices[5]) + (slices[6] + slices[7])
+    total = low + high
+    for k in range(8):
+        line[k] = total
+
+
+def line_sums(base, slices):
+    one = jax.ShapeDtypeStruct(slices.shape[1:], F)
+    return pl.pallas_call(
+        line_kernel,
+        out_shape=(one, one, jax.ShapeDtypeStruct(slices.shape, F)),
+        in_specs=[SM, VM],
+        out_specs=(VM, VM, VM),
+        compiler_params=pltpu.CompilerParams(vmem_limit_bytes=LIMIT),
+    )(base, slices)
+
+
 def exchange(x, axes):
     return lax.all_to_all(x, axes, 0, 0)
 
@@ -355,25 +382,19 @@
     size = lax.axis_size(leaf)
     rows = points.shape[0]
     packed = jnp.concatenate([probes.T, points.T], axis=0)
-    up = [(i, i + 1) for i in range(size - 1)]
-    below = lax.ppermute(packed, leaf, up)
-    above = lax.ppermute(packed, leaf, [(b, a) for a, b in up])
+    across = [(i, (i + (1 if i % 2 else -1)) % size) for i in range(size)]
+    far = lax.ppermute(packed, leaf, across)
+    near = lax.ppermute(packed, leaf, [(i, i ^ 1) for i in range(size)])
     base = (lax.axis_index(leaf) * BLOCKS).astype(jnp.int32).reshape(1)
     part, sides, ids, end = own_tiles(base, near_list, near_count, packed)
-    turned, send = halo_tiles(ids, end, below, above, sides, part)
+    turned, send = halo_tiles(ids, end, near, far, sides, part)
     samples = turned.T
     columns = exchange(send, "x")
     pieces = gram(columns).reshape(8, 40, 128)
     level1 = jnp.sum(exchange(pieces, ("c", "x")), axis=0)
     along_z = to_all(level1, "z", 8)
-    z = lax.axis_index("z")
-    pair = lax.dynamic_slice_in_dim(along_z, z // 2 * 2, 2, 0)
-    four = lax.dynamic_slice_in_dim(along_z, z // 4 * 4, 4, 0)
-    level2 = jnp.sum(pair, axis=0)
-    level3 = jnp.sum(four, axis=0)
-    line = jnp.sum(along_z, axis=0)
-    level2, level3, line = lax.optimization_barrier((level2, level3, line))
-    along_y = to_all(line, "y", 8)
+    level2, level3, line = line_sums(base, along_z)
+    along_y = exchange(line, "y")
     root = jnp.sum(along_y, axis=0)
     slices = to_all(jnp.stack([level1, level2, level3, root]), ("c", "x"), 8)
     scales = [1.0 / (rows * 2 ** (l + 1)) for l in range(LEVELS)] + [1.0 / (rows * size)]

time: 108 us -> 108 us (level)
  blocking collectives: 49.8 us -> 61.8 us
  waiting for transfers between devices: 8.63 us -> 0.01 us
  starting transfers between devices: 22.7 us -> 16.7 us
  Pallas kernels: 23.5 us -> 26.4 us
    all_to_all x1 -> x0, starting transfers between devices: 12.6 us -> none  [exchange(): return lax.all_to_all(x, axes, 0, 0)]
    all_to_all x4 -> x5, blocking collectives: 49.8 us -> 61.8 us  [exchange(): return lax.all_to_all(x, axes, 0, 0)]
    all_to_all x1 -> x0, waiting for transfers between devices: 8.62 us -> none  [exchange(): return lax.all_to_all(x, axes, 0, 0)]
    ppermute x2, starting transfers between devices: 10.1 us -> 16.7 us  [the longest x1 11.3 us: body(): near = lax.ppermute(packed, leaf, [(i, i ^ 1) for i in range(size)])]
    pallas_call x1, Pallas kernels: 6.64 us -> 8.75 us  [own_tiles(): pl.pallas_call(own_kernel, out_shape=(jax.ShapeDtypeStruct((BLOCKS, 64, B...]
  transfers between devices with their start and end apart: 3 -> 2, of which waited for: 1 -> 0; matrix products, arithmetic and copies ran while one was open for 0% -> 0% of each run, Pallas kernels for 6% -> 8%
where the time goes in v4:
time: 108 us
  blocking collectives  61.8 us (57%)
  Pallas kernels  26.4 us (24%)
  starting transfers between devices  16.7 us (15%)
  other arithmetic  1.1 us (1%)
    all_to_all x5, blocking collectives, exchange(): return lax.all_to_all(x, axes, 0, 0)  61.8 us
    ppermute x1, starting transfers between devices, body(): near = lax.ppermute(packed, leaf, [(i, i ^ 1) for i in range(size)])  11.3 us
    pallas_call x1, Pallas kernels, factors(): pl.pallas_call(functools.partial(factor_kernel, scales), out_shape=(jax.S...  9.53 us
    pallas_call x1, Pallas kernels, own_tiles(): pl.pallas_call(own_kernel, out_shape=(jax.ShapeDtypeStruct((BLOCKS, 64, B...  8.75 us
    pallas_call x1, Pallas kernels, halo_tiles(): pl.pallas_call(halo_kernel, out_shape=(jax.ShapeDtypeStruct((64, BLOCKS *...  7.46 us
    ppermute x1, starting transfers between devices, body(): far = lax.ppermute(packed, leaf, across)  5.39 us
  transfers between devices with their start and end apart: 2, of which 0 were waited for; matrix products, arithmetic and copies ran while one was open for 0% of the time, Pallas kernels for 8%

profile of v4, /device:TPU:1, one launch (start us, length us, event | category | flops | bytes accessed | tf_op | source)
XLA Modules:
  0.0 107.5 jit_solution(9199808575079202338)
XLA Ops:
  0.6 1.1 pad_maximum_fusion.own_ref
  1.7 5.4 %collective-permute-start.1 = (bf16[128,2048]{1,0:T(8,128)(2,1)S(1)}, bf16[128,2048]{1,0:T(8,128)(2,1)S(1)}, u32[]{:S(2)}, u32[]{:S(2)}) collective-permute-start(bf16[128,2048]{1,0:T(8,128)(2,1)S(1)} %pad_maximum_fusion.own_ref), channel_id=1, source_target_pairs={{0,508},{4,8},{8,4},{12,16},{16,12},{20,24},{24,20},{28,32},{32,28... | collective-permute-start | bytes 1572872 | tf_op jit(solution)/shard_map/ppermute | solution.py:386
  7.1 11.3 %collective-permute-start = (bf16[128,2048]{1,0:T(8,128)(2,1)S(1)}, bf16[128,2048]{1,0:T(8,128)(2,1)S(1)}, u32[]{:S(2)}, u32[]{:S(2)}) collective-permute-start(bf16[128,2048]{1,0:T(8,128)(2,1)S(1)} %pad_maximum_fusion.own_ref), channel_id=1, source_target_pairs={{0,4},{4,0},{8,12},{12,8},{16,20},{20,16},{24,28},{28,24},{32,36},... | collective-permute-start | bytes 1572872 | tf_op jit(solution)/shard_map/ppermute | solution.py:387
  18.4 0.0 copy-start
  18.4 0.0 copy-start.1
  18.5 0.7 copy-done
  19.1 0.0 copy-done.1
  19.1 8.7 %shard_map.67 = (f32[8,64,256]{2,1,0:T(8,128)S(1)}, bf16[8,128,256]{2,1,0:T(8,128)(2,1)S(1)}, s32[2,152]{1,0:T(2,128)S(1)}, s32[1]{0:T(128)}) custom-call(s32[1]{0:T(128)} %bitcast.base_ref, s32[8,16]{1,0:T(8,128)S(1)} %copy-done, s32[8]{0:T(128)S(1)} %copy-done.1, bf16[128,2048]{1,0:T(8,128)(2,1)S(1)} %pad_maximum_fusion.own_ref), custom_call_target="tpu_custom_call" | custom-call | flops 3221225472 | bytes 4194304 | tf_op jit(solution)/shard_map/pallas_call | solution.py:162
  27.9 0.0 collective-permute-done.1.far_ref
  27.9 0.0 collective-permute-done.near_ref
  27.9 7.5 %shard_map.68 = (f32[64,2048]{1,0:T(8,128)}, f32[4,2,64,256]{3,2,1,0:T(8,128)S(1)}) custom-call(s32[2,152]{1,0:T(2,128)S(1)} %get-tuple-element.14.ids, s32[1]{0:T(128)} %get-tuple-element.15.end_ref, bf16[128,2048]{1,0:T(8,128)(2,1)S(1)} %collective-permute-done.near_ref, bf16[128,2048]{1,0:T(8,128)(2,1)S(1)} %collective-permute-done.1.far_ref, ...), custom_call_target="tpu_custom_call" | custom-call | flops 3221225472 | bytes 4194304 | tf_op jit(solution)/shard_map/pallas_call | solution.py:185
  35.4 12.4 %all_to_all.25.columns_ref = f32[4,2,64,256]{3,2,1,0:T(8,128)S(1)} all-to-all(f32[4,2,64,256]{3,2,1,0:T(8,128)S(1)} %get-tuple-element.19), channel_id=1, replica_groups=mesh['y'=8,'z'=8,'c'=2,'x'=4] {'x'}, dimensions={0} | all-to-all | bytes 1048576 | tf_op jit(solution)/shard_map/all_to_all | solution.py:373
  47.8 0.7 shard_map.69
  48.5 7.9 %all_to_all.26 = f32[8,40,128]{2,1,0:T(8,128)S(1)} all-to-all(f32[8,40,128]{2,1,0:T(8,128)S(1)} %bitcast.9), channel_id=1, replica_groups=mesh['y'=8,'z'=8,'c'=2,'x'=4] {'c','x'}, dimensions={0} | all-to-all | bytes 327680 | tf_op jit(solution)/shard_map/all_to_all | solution.py:373
  56.4 11.6 %all_to_all.27.slices = f32[8,40,128]{2,1,0:T(8,128)S(1)} all-to-all(f32[8,40,128]{2,1,0:T(8,128)S(1)} %broadcast_in_dim.4), channel_id=1, replica_groups=mesh['y'=8,'z'=8,'c'=2,'x'=4] {'z'}, dimensions={0} | all-to-all | bytes 327680 | tf_op jit(solution)/shard_map/all_to_all | solution.py:373
  68.0 13.4 %all_to_all.28 = f32[8,40,128]{2,1,0:T(8,128)S(1)} all-to-all(f32[8,40,128]{2,1,0:T(8,128)S(1)} %get-tuple-element.22), channel_id=1, replica_groups=mesh['y'=8,'z'=8,'c'=2,'x'=4] {'y'}, dimensions={0} | all-to-all | bytes 327680 | tf_op jit(solution)/shard_map/all_to_all | solution.py:373
  81.4 16.6 %all_to_all.29.slices_ref = f32[8,4,40,128]{3,2,1,0:T(8,128)S(1)} all-to-all(f32[8,4,40,128]{3,2,1,0:T(8,128)S(1)} %broadcast_in_dim.5), channel_id=1, replica_groups=mesh['y'=8,'z'=8,'c'=2,'x'=4] {'c','x'}, dimensions={0} | all-to-all | bytes 1310720 | tf_op jit(solution)/shard_map/all_to_all | solution.py:373
  98.0 9.5 %shard_map.71 = (f32[1,3,256,256]{3,2,1,0:T(8,128)}, f32[256,256]{1,0:T(8,128)}) custom-call(f32[8,4,40,128]{3,2,1,0:T(8,128)S(1)} %all_to_all.29.slices_ref), custom_call_target="tpu_custom_call" | custom-call | tf_op jit(solution)/shard_map/pallas_call | solution.py:335
  (6 shorter events, 0.1 us)
Async XLA Ops:
  1.7 26.2 %collective-permute-start.1 = (bf16[128,2048]{1,0:T(8,128)(2,1)S(1)}, bf16[128,2048]{1,0:T(8,128)(2,1)S(1)}, u32[]{:S(2)}, u32[]{:S(2)}) collective-permute-start(bf16[128,2048]{1,0:T(8,128)(2,1)S(1)} %pad_maximum_fusion.own_ref), channel_id=1, source_target_pairs={{0,508},{4,8},{8,4},{12,16},{16,12},{20,24},{24,20},{28,32},{32,28... | collective-permute-start | bytes 1572872 | tf_op jit(solution)/shard_map/ppermute | solution.py:386
  7.1 20.8 %collective-permute-start = (bf16[128,2048]{1,0:T(8,128)(2,1)S(1)}, bf16[128,2048]{1,0:T(8,128)(2,1)S(1)}, u32[]{:S(2)}, u32[]{:S(2)}) collective-permute-start(bf16[128,2048]{1,0:T(8,128)(2,1)S(1)} %pad_maximum_fusion.own_ref), channel_id=1, source_target_pairs={{0,4},{4,0},{8,12},{12,8},{16,20},{20,16},{24,28},{28,24},{32,36},... | collective-permute-start | bytes 1572872 | tf_op jit(solution)/shard_map/ppermute | solution.py:387
  18.4 0.7 copy-start
  18.4 0.7 copy-start.1

commit v5 on v4

--- a/solution.py
+++ b/solution.py
@@ -12,7 +12,7 @@
 BOX = 256
 SLOTS = 16
 GROUP = 8
-ENTRIES = BLOCKS * SLOTS + 3 * GROUP
+ENTRIES = BLOCKS * SLOTS + 4 * GROUP
 BF = jnp.bfloat16
 F = jnp.float32
 NN = (((1,), (0,)), ((), ()))
@@ -79,28 +79,27 @@
     return lax.fori_loop(0, BLOCKS, of_box, (jnp.int32(GROUP), jnp.int32(GROUP)))
 
 
-def run_list(end, ids, own, other, probes, cross, parts, total):
+def run_list(end, ids, own, other, probes, parts, total):
+    parts[...] = jnp.zeros_like(parts)
+
     def step(t, _):
         at = [t * GROUP + k for k in range(GROUP)]
         for k in range(GROUP):
-            cross[k] = dot(other[ids[1, at[k]]], own[ids[0, at[k]]], NN)
-        for k in range(GROUP):
-            tile = jnp.exp2(cross[k] * LOG2E_OVER_32)
+            left = probes[ids[1, at[k] - GROUP]]
+            i = ids[0, at[k] - GROUP]
+            total[i] = total[i] + dot(jnp.concatenate([left, left], axis=1), parts[k], NN)
+            tile = jnp.exp2(dot(other[ids[1, at[k]]], own[ids[0, at[k]]], NN) * LOG2E_OVER_32)
             h = tile.astype(BF)
             parts[k, 0:BOX] = h
             parts[k, BOX:2 * BOX] = (tile - h.astype(F)).astype(BF)
-        for k in range(GROUP):
-            left = probes[ids[1, at[k]]]
-            i = ids[0, at[k]]
-            total[i] = total[i] + dot(jnp.concatenate([left, left], axis=1), parts[k], NN)
         return 0
 
-    lax.fori_loop(1, (end + GROUP - 1) // GROUP, step, 0)
+    lax.fori_loop(1, (end + GROUP - 1) // GROUP + 1, step, 0)
 
 
 def own_kernel(
     base_ref, list_hbm, count_hbm, own_ref, total, sides, halo_ids, halo_end,
-    other, probes, cross, parts, ids, list_ref, count_ref, sems,
+    other, probes, parts, ids, list_ref, count_ref, sems,
 ):
     copies = [
         pltpu.make_async_copy(list_hbm, list_ref, sems.at[0]),
@@ -121,14 +120,14 @@
     end, end_halo = build_lists(base_ref[0], list_ref, count_ref, ids, halo_ids)
     halo_end[0] = end_halo
     for k in range(GROUP):
-        ids[0, end + k] = 0
-        ids[1, end + k] = BLOCKS
-        halo_ids[0, end_halo + k] = 0
-        halo_ids[1, end_halo + k] = 2 * BLOCKS
-    run_list(end, ids, sides, other, probes, cross, parts, total)
-
-
-def halo_kernel(ids, end_ref, near_ref, far_ref, sides, part, turned, send, other, probes, cross, parts, total):
+        for start_ids, null, last in ((ids, BLOCKS, end), (halo_ids, 2 * BLOCKS, end_halo)):
+            for e in (k, last + k, last + GROUP + k):
+                start_ids[0, e] = 0
+                start_ids[1, e] = null
+    run_list(end, ids, sides, other, probes, parts, total)
+
+
+def halo_kernel(ids, end_ref, near_ref, far_ref, sides, part, turned, send, other, probes, parts, total):
     for q, ref in enumerate((near_ref, far_ref)):
         for b in range(BLOCKS):
             box = ref[:, BOX * b:BOX * b + BOX]
@@ -137,7 +136,7 @@
     other[2 * BLOCKS] = jnp.zeros((BOX, 128), BF)
     probes[2 * BLOCKS] = jnp.zeros((64, BOX), BF)
     total[...] = part[...]
-    run_list(end_ref[0], ids, sides, other, probes, cross, parts, total)
+    run_list(end_ref[0], ids, sides, other, probes, parts, total)
     for b in range(BLOCKS):
         turned[:, BOX * b:BOX * b + BOX] = total[b]
         send[b // 2, b % 2] = total[b]
@@ -147,7 +146,6 @@
     return [
         pltpu.VMEM((boxes + 1, BOX, 128), BF),
         pltpu.VMEM((boxes + 1, 64, BOX), BF),
-        pltpu.VMEM((GROUP, BOX, BOX), F),
         pltpu.VMEM((GROUP, 2 * BOX, BOX), BF),
     ]
 
@@ -274,28 +272,27 @@
     return [jnp.concatenate([jnp.concatenate(v, axis=1) for v in p], axis=0) for p in part]
 
 
+def products(rows, lanes):
+    h, m, l = split3(rows)
+    left = jnp.concatenate([h, h, m, h, m, l], axis=0)[:, :lanes]
+    return dot(left, jnp.concatenate([h, m, h, l, m, h], axis=0), TN)
+
+
 def factor(n, work, upper):
-    for half in range(2):
-        c0 = 128 * half
+    for c0 in (0, 128):
         for k in range(4):
             r0 = c0 + 32 * k
             rows = panel_step([work[b, r0:r0 + 32, c0:256] for b in range(n)], 32 * k, 256 - c0)
             for b in range(n):
                 upper[b, r0:r0 + 32, c0:256] = rows[b]
             lo = r0 + 32
-            if lo == 256:
-                break
             for b in range(n):
-                h, m, l = split3(rows[b])
-                left = jnp.concatenate([h, h, m, h, m, l], axis=0)
-                right = jnp.concatenate([h, m, h, l, m, h], axis=0)
-                update = dot(left, right, TN)
-                if half == 0:
-                    if lo < 128:
-                        work[b, lo:128, :] = work[b, lo:128, :] - update[lo:128, :]
-                    work[b, 128:256, 128:256] = work[b, 128:256, 128:256] - update[128:256, 128:256]
-                else:
-                    work[b, lo:256, 128:256] = work[b, lo:256, 128:256] - update[lo - 128:128, :]
+                if k < 3:
+                    update = products(rows[b], 128)
+                    work[b, lo:c0 + 128, c0:256] = work[b, lo:c0 + 128, c0:256] - update[lo - c0:, :]
+                elif c0 == 0:
+                    update = products(upper[b, 0:128, 128:256], 128)
+                    work[b, 128:256, 128:256] = work[b, 128:256, 128:256] - update
 
 
 def factor_kernel(scales, slices_ref, nodes_ref, root_ref, work, upper):

time: 108 us -> 105 us (0.972)
  Pallas kernels: 26.4 us -> 22.2 us
  blocking collectives: 61.8 us -> 63.4 us
    pallas_call x1, Pallas kernels: 8.75 us -> 5.86 us  [own_tiles(): pl.pallas_call(own_kernel, out_shape=(jax.ShapeDtypeStruct((BLOCKS, 64, B...]
    all_to_all x5, blocking collectives: 61.8 us -> 63.4 us  [exchange(): return lax.all_to_all(x, axes, 0, 0)]
  transfers between devices with their start and end apart: 2 -> 2, of which waited for: 0 -> 0; matrix products, arithmetic and copies ran while one was open for 0% -> 0% of each run, Pallas kernels for 8% -> 6%
where the time goes in v5:
time: 105 us
  blocking collectives  63.4 us (60%)
  Pallas kernels  22.2 us (21%)
  starting transfers between devices  16.7 us (16%)
  other arithmetic  1.1 us (1%)
    all_to_all x5, blocking collectives, exchange(): return lax.all_to_all(x, axes, 0, 0)  63.4 us
    ppermute x1, starting transfers between devices, body(): near = lax.ppermute(packed, leaf, [(i, i ^ 1) for i in range(size)])  11.3 us
    pallas_call x1, Pallas kernels, factors(): pl.pallas_call(functools.partial(factor_kernel, scales), out_shape=(jax.S...  8.97 us
    pallas_call x1, Pallas kernels, halo_tiles(): pl.pallas_call(halo_kernel, out_shape=(jax.ShapeDtypeStruct((64, BLOCKS *...  6.66 us
    pallas_call x1, Pallas kernels, own_tiles(): pl.pallas_call(own_kernel, out_shape=(jax.ShapeDtypeStruct((BLOCKS, 64, B...  5.86 us
    ppermute x1, starting transfers between devices, body(): far = lax.ppermute(packed, leaf, across)  5.39 us
  transfers between devices with their start and end apart: 2, of which 0 were waited for; matrix products, arithmetic and copies ran while one was open for 0% of the time, Pallas kernels for 6%

profile of v5, /device:TPU:1, one launch (start us, length us, event | category | flops | bytes accessed | tf_op | source)
XLA Modules:
  0.0 104.9 jit_solution(4469604499784424343)
XLA Ops:
  0.6 1.1 %pad_maximum_fusion.own_ref = bf16[128,2048]{1,0:T(8,128)(2,1)S(1)} fusion(bf16[64,2048]{1,0:T(8,128)(2,1)} %bitcast.12, bf16[64,2048]{1,0:T(8,128)(2,1)} %bitcast.13), kind=kLoop, calls=%fused_computation | loop fusion | flops 1048576 | bytes 1048576 | tf_op jit(solution)/shard_map/concatenate | solution.py:381
  1.7 5.4 %collective-permute-start.1 = (bf16[128,2048]{1,0:T(8,128)(2,1)S(1)}, bf16[128,2048]{1,0:T(8,128)(2,1)S(1)}, u32[]{:S(2)}, u32[]{:S(2)}) collective-permute-start(bf16[128,2048]{1,0:T(8,128)(2,1)S(1)} %pad_maximum_fusion.own_ref), channel_id=1, source_target_pairs={{0,508},{4,8},{8,4},{12,16},{16,12},{20,24},{24,20},{28,32},{32,28... | collective-permute-start | bytes 1572872 | tf_op jit(solution)/shard_map/ppermute | solution.py:383
  7.1 11.3 %collective-permute-start = (bf16[128,2048]{1,0:T(8,128)(2,1)S(1)}, bf16[128,2048]{1,0:T(8,128)(2,1)S(1)}, u32[]{:S(2)}, u32[]{:S(2)}) collective-permute-start(bf16[128,2048]{1,0:T(8,128)(2,1)S(1)} %pad_maximum_fusion.own_ref), channel_id=1, source_target_pairs={{0,4},{4,0},{8,12},{12,8},{16,20},{20,16},{24,28},{28,24},{32,36},... | collective-permute-start | bytes 1572872 | tf_op jit(solution)/shard_map/ppermute | solution.py:384
  18.4 0.0 copy-start
  18.4 0.0 copy-start.1
  18.5 0.7 copy-done
  19.1 0.0 copy-done.1
  19.1 5.9 %shard_map.67 = (f32[8,64,256]{2,1,0:T(8,128)S(1)}, bf16[8,128,256]{2,1,0:T(8,128)(2,1)S(1)}, s32[2,160]{1,0:T(2,128)S(1)}, s32[1]{0:T(128)}) custom-call(s32[1]{0:T(128)} %bitcast.base_ref, s32[8,16]{1,0:T(8,128)S(1)} %copy-done, s32[8]{0:T(128)S(1)} %copy-done.1, bf16[128,2048]{1,0:T(8,128)(2,1)S(1)} %pad_maximum_fusion.own_ref), custom_call_target="tpu_custom_call" | custom-call | flops 3221225472 | bytes 4194304 | tf_op jit(solution)/shard_map/pallas_call | solution.py:160
  25.0 0.0 collective-permute-done.1.far_ref
  25.0 0.0 collective-permute-done.near_ref
  25.0 6.7 %shard_map.68 = (f32[64,2048]{1,0:T(8,128)}, f32[4,2,64,256]{3,2,1,0:T(8,128)S(1)}) custom-call(s32[2,160]{1,0:T(2,128)S(1)} %get-tuple-element.14.ids, s32[1]{0:T(128)} %get-tuple-element.15.end_ref, bf16[128,2048]{1,0:T(8,128)(2,1)S(1)} %collective-permute-done.near_ref, bf16[128,2048]{1,0:T(8,128)(2,1)S(1)} %collective-permute-done.1.far_ref, ...), custom_call_target="tpu_custom_call" | custom-call | flops 3221225472 | bytes 4194304 | tf_op jit(solution)/shard_map/pallas_call | solution.py:183
  31.7 12.3 %all_to_all.25.columns_ref = f32[4,2,64,256]{3,2,1,0:T(8,128)S(1)} all-to-all(f32[4,2,64,256]{3,2,1,0:T(8,128)S(1)} %get-tuple-element.19), channel_id=1, replica_groups=mesh['y'=8,'z'=8,'c'=2,'x'=4] {'x'}, dimensions={0} | all-to-all | bytes 1048576 | tf_op jit(solution)/shard_map/all_to_all | solution.py:370
  44.0 0.7 shard_map.69
  44.6 9.8 %all_to_all.26 = f32[8,40,128]{2,1,0:T(8,128)S(1)} all-to-all(f32[8,40,128]{2,1,0:T(8,128)S(1)} %bitcast.9), channel_id=1, replica_groups=mesh['y'=8,'z'=8,'c'=2,'x'=4] {'c','x'}, dimensions={0} | all-to-all | bytes 327680 | tf_op jit(solution)/shard_map/all_to_all | solution.py:370
  54.5 11.5 %all_to_all.27.slices = f32[8,40,128]{2,1,0:T(8,128)S(1)} all-to-all(f32[8,40,128]{2,1,0:T(8,128)S(1)} %broadcast_in_dim.4), channel_id=1, replica_groups=mesh['y'=8,'z'=8,'c'=2,'x'=4] {'z'}, dimensions={0} | all-to-all | bytes 327680 | tf_op jit(solution)/shard_map/all_to_all | solution.py:370
  66.1 13.2 %all_to_all.28 = f32[8,40,128]{2,1,0:T(8,128)S(1)} all-to-all(f32[8,40,128]{2,1,0:T(8,128)S(1)} %get-tuple-element.22), channel_id=1, replica_groups=mesh['y'=8,'z'=8,'c'=2,'x'=4] {'y'}, dimensions={0} | all-to-all | bytes 327680 | tf_op jit(solution)/shard_map/all_to_all | solution.py:370
  79.3 16.6 %all_to_all.29.slices_ref = f32[8,4,40,128]{3,2,1,0:T(8,128)S(1)} all-to-all(f32[8,4,40,128]{3,2,1,0:T(8,128)S(1)} %broadcast_in_dim.5), channel_id=1, replica_groups=mesh['y'=8,'z'=8,'c'=2,'x'=4] {'c','x'}, dimensions={0} | all-to-all | bytes 1310720 | tf_op jit(solution)/shard_map/all_to_all | solution.py:370
  95.9 9.0 %shard_map.71 = (f32[1,3,256,256]{3,2,1,0:T(8,128)}, f32[256,256]{1,0:T(8,128)}) custom-call(f32[8,4,40,128]{3,2,1,0:T(8,128)S(1)} %all_to_all.29.slices_ref), custom_call_target="tpu_custom_call" | custom-call | tf_op jit(solution)/shard_map/pallas_call | solution.py:332
  (6 shorter events, 0.1 us)
Async XLA Ops:
  1.7 23.3 %collective-permute-start.1 = (bf16[128,2048]{1,0:T(8,128)(2,1)S(1)}, bf16[128,2048]{1,0:T(8,128)(2,1)S(1)}, u32[]{:S(2)}, u32[]{:S(2)}) collective-permute-start(bf16[128,2048]{1,0:T(8,128)(2,1)S(1)} %pad_maximum_fusion.own_ref), channel_id=1, source_target_pairs={{0,508},{4,8},{8,4},{12,16},{16,12},{20,24},{24,20},{28,32},{32,28... | collective-permute-start | bytes 1572872 | tf_op jit(solution)/shard_map/ppermute | solution.py:383
  7.1 17.9 %collective-permute-start = (bf16[128,2048]{1,0:T(8,128)(2,1)S(1)}, bf16[128,2048]{1,0:T(8,128)(2,1)S(1)}, u32[]{:S(2)}, u32[]{:S(2)}) collective-permute-start(bf16[128,2048]{1,0:T(8,128)(2,1)S(1)} %pad_maximum_fusion.own_ref), channel_id=1, source_target_pairs={{0,4},{4,0},{8,12},{12,8},{16,20},{20,16},{24,28},{28,24},{32,36},... | collective-permute-start | bytes 1572872 | tf_op jit(solution)/shard_map/ppermute | solution.py:384
  18.4 0.7 copy-start
  18.4 0.7 copy-start.1

commit v6 on v5

--- a/solution.py
+++ b/solution.py
@@ -12,7 +12,7 @@
 BOX = 256
 SLOTS = 16
 GROUP = 8
-ENTRIES = BLOCKS * SLOTS + 4 * GROUP
+ENTRIES = BLOCKS * SLOTS + 3 * GROUP
 BF = jnp.bfloat16
 F = jnp.float32
 NN = (((1,), (0,)), ((), ()))
@@ -80,21 +80,31 @@
 
 
 def run_list(end, ids, own, other, probes, parts, total):
-    parts[...] = jnp.zeros_like(parts)
+    def make(t, k):
+        e = t * GROUP + k
+        tile = jnp.exp2(dot(other[ids[1, e]], own[ids[0, e]], NN) * LOG2E_OVER_32)
+        h = tile.astype(BF)
+        parts[k, 0:BOX] = h
+        parts[k, BOX:2 * BOX] = (tile - h.astype(F)).astype(BF)
+
+    def use(t, k):
+        e = t * GROUP + k
+        left = probes[ids[1, e]]
+        i = ids[0, e]
+        total[i] = total[i] + dot(jnp.concatenate([left, left], axis=1), parts[k], NN)
 
     def step(t, _):
-        at = [t * GROUP + k for k in range(GROUP)]
         for k in range(GROUP):
-            left = probes[ids[1, at[k] - GROUP]]
-            i = ids[0, at[k] - GROUP]
-            total[i] = total[i] + dot(jnp.concatenate([left, left], axis=1), parts[k], NN)
-            tile = jnp.exp2(dot(other[ids[1, at[k]]], own[ids[0, at[k]]], NN) * LOG2E_OVER_32)
-            h = tile.astype(BF)
-            parts[k, 0:BOX] = h
-            parts[k, BOX:2 * BOX] = (tile - h.astype(F)).astype(BF)
+            use(t - 1, k)
+            make(t, k)
         return 0
 
-    lax.fori_loop(1, (end + GROUP - 1) // GROUP + 1, step, 0)
+    last = jnp.maximum((end - 1) // GROUP, 1)
+    for k in range(GROUP):
+        make(1, k)
+    lax.fori_loop(2, last + 1, step, 0)
+    for k in range(GROUP):
+        use(last, k)
 
 
 def own_kernel(
@@ -120,14 +130,13 @@
     end, end_halo = build_lists(base_ref[0], list_ref, count_ref, ids, halo_ids)
     halo_end[0] = end_halo
     for k in range(GROUP):
-        for start_ids, null, last in ((ids, BLOCKS, end), (halo_ids, 2 * BLOCKS, end_halo)):
-            for e in (k, last + k, last + GROUP + k):
-                start_ids[0, e] = 0
-                start_ids[1, e] = null
+        for to, null, last in ((ids, BLOCKS, end), (halo_ids, 2 * BLOCKS, end_halo)):
+            to[0, last + k] = 0
+            to[1, last + k] = null
     run_list(end, ids, sides, other, probes, parts, total)
 
 
-def halo_kernel(ids, end_ref, near_ref, far_ref, sides, part, turned, send, other, probes, parts, total):
+def halo_kernel(ids, end_ref, near_ref, far_ref, sides, part, send, other, probes, parts, total):
     for q, ref in enumerate((near_ref, far_ref)):
         for b in range(BLOCKS):
             box = ref[:, BOX * b:BOX * b + BOX]
@@ -138,7 +147,6 @@
     total[...] = part[...]
     run_list(end_ref[0], ids, sides, other, probes, parts, total)
     for b in range(BLOCKS):
-        turned[:, BOX * b:BOX * b + BOX] = total[b]
         send[b // 2, b % 2] = total[b]
 
 
@@ -182,12 +190,9 @@
 def halo_tiles(ids, end, near, far, sides, part):
     return pl.pallas_call(
         halo_kernel,
-        out_shape=(
-            jax.ShapeDtypeStruct((64, BLOCKS * BOX), F),
-            jax.ShapeDtypeStruct((BLOCKS // 2, 2, 64, BOX), F),
-        ),
+        out_shape=jax.ShapeDtypeStruct((BLOCKS // 2, 2, 64, BOX), F),
         in_specs=[SM, SM] + [VM] * 4,
-        out_specs=(VM, VM),
+        out_specs=VM,
         scratch_shapes=list_scratch(2 * BLOCKS) + [pltpu.VMEM((BLOCKS, 64, BOX), F)],
         compiler_params=pltpu.CompilerParams(vmem_limit_bytes=LIMIT),
         cost_estimate=tiles_cost(),
@@ -278,7 +283,7 @@
     return dot(left, jnp.concatenate([h, m, h, l, m, h], axis=0), TN)
 
 
-def factor(n, work, upper):
+def factor(n, work, upper, beside):
     for c0 in (0, 128):
         for k in range(4):
             r0 = c0 + 32 * k
@@ -293,13 +298,24 @@
                 elif c0 == 0:
                     update = products(upper[b, 0:128, 128:256], 128)
                     work[b, 128:256, 128:256] = work[b, 128:256, 128:256] - update
-
-
-def factor_kernel(scales, slices_ref, nodes_ref, root_ref, work, upper):
+            if c0:
+                beside(k)
+
+
+def factor_kernel(scales, slices_ref, send_ref, turned, nodes, root, work, upper, left, right, sems):
     n = len(scales)
+    copies = []
+
+    def copy(src, dst):
+        copies.append(pltpu.make_async_copy(src, dst, sems.at[len(copies)]))
+        copies[-1].start()
+
+    for b in range(BLOCKS):
+        copy(send_ref.at[b // 2, b % 2], turned.at[:, pl.ds(BOX * b, BOX)])
     ri = lax.broadcasted_iota(jnp.int32, (128, 128), 0)
     ci = lax.broadcasted_iota(jnp.int32, (128, 128), 1)
     eye = jnp.where(ri == ci, 1.0, 0.0)
+    below = ri >= ci
     for b in range(n):
         t = jnp.concatenate([slices_ref[r, b] for r in range(8)], axis=0) * scales[b]
         work[b, 0:64, 0:128] = t[0:64] + eye[0:64]
@@ -308,38 +324,44 @@
         work[b, 64:128, 128:256] = t[128:192]
         work[b, 128:192, 128:256] = t[192:256] + eye[0:64]
         work[b, 192:256, 128:256] = pltpu.roll(t[256:320], 64, 1) + eye[64:128]
-    factor(n, work, upper)
-    below = ri >= ci
-    for b in range(n):
-        first = jnp.where(below, upper[b, 0:128, 0:128].T, 0.0)
-        cross = upper[b, 0:128, 128:256].T
-        second = jnp.where(below, upper[b, 128:256, 128:256].T, 0.0)
-        low = jnp.concatenate(
-            [
-                jnp.concatenate([first, jnp.zeros((128, 128), F)], axis=1),
-                jnp.concatenate([cross, second], axis=1),
-            ],
-            axis=0,
-        )
-        if b < LEVELS:
-            nodes_ref[0, b] = low
-        else:
-            root_ref[...] = low
-
-
-def factors(slices, scales):
+
+    def place(b, half):
+        columns = pl.ds(128 * half, 128)
+        return nodes.at[0, b, :, columns] if b < LEVELS else root.at[:, columns]
+
+    def beside(k):
+        for b in range(n):
+            if k == b // 2:
+                left[b, 0:128] = jnp.where(below, upper[b, 0:128, 0:128].T, 0.0)
+                left[b, 128:256] = upper[b, 0:128, 128:256].T
+                copy(left.at[b], place(b, 0))
+            if k == 3:
+                right[b, 0:128] = jnp.zeros((128, 128), F)
+                right[b, 128:256] = jnp.where(below, upper[b, 128:256, 128:256].T, 0.0)
+                copy(right.at[b], place(b, 1))
+
+    factor(n, work, upper, beside)
+    for c in copies:
+        c.wait()
+
+
+def factors(slices, send, scales):
     n = len(scales)
+    any_place = pl.BlockSpec(memory_space=pl.ANY)
     return pl.pallas_call(
         functools.partial(factor_kernel, scales),
         out_shape=(
+            jax.ShapeDtypeStruct((64, BLOCKS * BOX), F),
             jax.ShapeDtypeStruct((1, LEVELS, 256, 256), F),
             jax.ShapeDtypeStruct((256, 256), F),
         ),
-        in_specs=[VM],
-        out_specs=(VM, VM),
-        scratch_shapes=[pltpu.VMEM((n, 256, 256), F)] * 2,
+        in_specs=[VM, VM],
+        out_specs=(any_place,) * 3,
+        scratch_shapes=[pltpu.VMEM((n, 256, 256), F)] * 2
+        + [pltpu.VMEM((n, 256, 128), F)] * 2
+        + [pltpu.SemaphoreType.DMA((BLOCKS + 2 * n,))],
         compiler_params=pltpu.CompilerParams(vmem_limit_bytes=LIMIT),
-    )(slices)
+    )(slices, send)
 
 
 def line_kernel(base_ref, slices, level2, level3, line):
@@ -384,8 +406,7 @@
     near = lax.ppermute(packed, leaf, [(i, i ^ 1) for i in range(size)])
     base = (lax.axis_index(leaf) * BLOCKS).astype(jnp.int32).reshape(1)
     part, sides, ids, end = own_tiles(base, near_list, near_count, packed)
-    turned, send = halo_tiles(ids, end, near, far, sides, part)
-    samples = turned.T
+    send = halo_tiles(ids, end, near, far, sides, part)
     columns = exchange(send, "x")
     pieces = gram(columns).reshape(8, 40, 128)
     level1 = jnp.sum(exchange(pieces, ("c", "x")), axis=0)
@@ -395,8 +416,8 @@
     root = jnp.sum(along_y, axis=0)
     slices = to_all(jnp.stack([level1, level2, level3, root]), ("c", "x"), 8)
     scales = [1.0 / (rows * 2 ** (l + 1)) for l in range(LEVELS)] + [1.0 / (rows * size)]
-    node_factors, root_factor = factors(slices, scales)
-    return samples, node_factors, root_factor
+    turned, node_factors, root_factor = factors(slices, send, scales)
+    return turned.T, node_factors, root_factor
 
 
 def solution(mesh):

time: 105 us -> 105 us (level)
  Pallas kernels: 22.2 us -> 20.2 us
  blocking collectives: 63.4 us -> 64.9 us
    pallas_call x1, Pallas kernels: 6.66 us -> 4.7 us  [halo_tiles(): pl.pallas_call(halo_kernel, out_shape=jax.ShapeDtypeStruct((BLOCKS // 2,...]
    all_to_all x5, blocking collectives: 63.4 us -> 64.9 us  [exchange(): return lax.all_to_all(x, axes, 0, 0)]
where the time goes in v6:
time: 105 us
  blocking collectives  64.9 us (62%)
  Pallas kernels  20.2 us (19%)
  starting transfers between devices  16.7 us (16%)
  other arithmetic  1.1 us (1%)
    all_to_all x5, blocking collectives, exchange(): return lax.all_to_all(x, axes, 0, 0)  64.9 us
    ppermute x1, starting transfers between devices, body(): near = lax.ppermute(packed, leaf, [(i, i ^ 1) for i in range(size)])  11.3 us
    pallas_call x1, Pallas kernels, factors(): pl.pallas_call(functools.partial(factor_kernel, scales), out_shape=(jax.S...  8.96 us
    pallas_call x1, Pallas kernels, own_tiles(): pl.pallas_call(own_kernel, out_shape=(jax.ShapeDtypeStruct((BLOCKS, 64, B...  5.88 us
    ppermute x1, starting transfers between devices, body(): far = lax.ppermute(packed, leaf, across)  5.39 us
    pallas_call x1, Pallas kernels, halo_tiles(): pl.pallas_call(halo_kernel, out_shape=jax.ShapeDtypeStruct((BLOCKS // 2,...  4.7 us
  transfers between devices with their start and end apart: 2, of which 0 were waited for; matrix products, arithmetic and copies ran while one was open for 0% of the time, Pallas kernels for 6%

profile of v6, /device:TPU:1, one launch (start us, length us, event | category | flops | bytes accessed | tf_op | source)
XLA Modules:
  0.0 104.6 jit_solution(10193798119190826396)
XLA Ops:
  0.6 1.1 %pad_maximum_fusion.own_ref = bf16[128,2048]{1,0:T(8,128)(2,1)S(1)} fusion(bf16[64,2048]{1,0:T(8,128)(2,1)} %bitcast.12, bf16[64,2048]{1,0:T(8,128)(2,1)} %bitcast.13), kind=kLoop, calls=%fused_computation | loop fusion | flops 1048576 | bytes 1048576 | tf_op jit(solution)/shard_map/concatenate | solution.py:403
  1.7 5.4 %collective-permute-start.1 = (bf16[128,2048]{1,0:T(8,128)(2,1)S(1)}, bf16[128,2048]{1,0:T(8,128)(2,1)S(1)}, u32[]{:S(2)}, u32[]{:S(2)}) collective-permute-start(bf16[128,2048]{1,0:T(8,128)(2,1)S(1)} %pad_maximum_fusion.own_ref), channel_id=1, source_target_pairs={{0,508},{4,8},{8,4},{12,16},{16,12},{20,24},{24,20},{28,32},{32,28... | collective-permute-start | bytes 1572872 | tf_op jit(solution)/shard_map/ppermute | solution.py:405
  7.1 11.3 %collective-permute-start = (bf16[128,2048]{1,0:T(8,128)(2,1)S(1)}, bf16[128,2048]{1,0:T(8,128)(2,1)S(1)}, u32[]{:S(2)}, u32[]{:S(2)}) collective-permute-start(bf16[128,2048]{1,0:T(8,128)(2,1)S(1)} %pad_maximum_fusion.own_ref), channel_id=1, source_target_pairs={{0,4},{4,0},{8,12},{12,8},{16,20},{20,16},{24,28},{28,24},{32,36},... | collective-permute-start | bytes 1572872 | tf_op jit(solution)/shard_map/ppermute | solution.py:406
  18.4 0.0 copy-start
  18.4 0.0 copy-start.1
  18.5 0.7 copy-done
  19.1 0.0 copy-done.1
  19.1 5.9 %shard_map.67 = (f32[8,64,256]{2,1,0:T(8,128)S(1)}, bf16[8,128,256]{2,1,0:T(8,128)(2,1)S(1)}, s32[2,152]{1,0:T(2,128)S(1)}, s32[1]{0:T(128)}) custom-call(s32[1]{0:T(128)} %bitcast.base_ref, s32[8,16]{1,0:T(8,128)S(1)} %copy-done, s32[8]{0:T(128)S(1)} %copy-done.1, bf16[128,2048]{1,0:T(8,128)(2,1)S(1)} %pad_maximum_fusion.own_ref), custom_call_target="tpu_custom_call" | custom-call | flops 3221225472 | bytes 4194304 | tf_op jit(solution)/shard_map/pallas_call | solution.py:168
  25.0 0.0 collective-permute-done.1.far_ref
  25.0 0.0 collective-permute-done.near_ref
  25.0 4.7 %shard_map.68.send_ref = f32[4,2,64,256]{3,2,1,0:T(8,128)S(1)} custom-call(s32[2,152]{1,0:T(2,128)S(1)} %get-tuple-element.13.ids, s32[1]{0:T(128)} %get-tuple-element.14.end_ref, bf16[128,2048]{1,0:T(8,128)(2,1)S(1)} %collective-permute-done.near_ref, bf16[128,2048]{1,0:T(8,128)(2,1)S(1)} %collective-permute-done.1.far_ref, ...), custom_call_target="tpu_custom_call" | custom-call | flops 3221225472 | bytes 4194304 | tf_op jit(solution)/shard_map/pallas_call | solution.py:191
  29.7 13.7 %all_to_all.25.columns_ref = f32[4,2,64,256]{3,2,1,0:T(8,128)S(1)} all-to-all(f32[4,2,64,256]{3,2,1,0:T(8,128)S(1)} %shard_map.68.send_ref), channel_id=1, replica_groups=mesh['y'=8,'z'=8,'c'=2,'x'=4] {'x'}, dimensions={0} | all-to-all | bytes 1048576 | tf_op jit(solution)/shard_map/all_to_all | solution.py:392
  43.5 0.7 shard_map.69
  44.2 8.3 %all_to_all.26 = f32[8,40,128]{2,1,0:T(8,128)S(1)} all-to-all(f32[8,40,128]{2,1,0:T(8,128)S(1)} %bitcast.9), channel_id=1, replica_groups=mesh['y'=8,'z'=8,'c'=2,'x'=4] {'c','x'}, dimensions={0} | all-to-all | bytes 327680 | tf_op jit(solution)/shard_map/all_to_all | solution.py:392
  52.5 11.5 %all_to_all.27.slices = f32[8,40,128]{2,1,0:T(8,128)S(1)} all-to-all(f32[8,40,128]{2,1,0:T(8,128)S(1)} %broadcast_in_dim.4), channel_id=1, replica_groups=mesh['y'=8,'z'=8,'c'=2,'x'=4] {'z'}, dimensions={0} | all-to-all | bytes 327680 | tf_op jit(solution)/shard_map/all_to_all | solution.py:392
  64.1 14.8 %all_to_all.28 = f32[8,40,128]{2,1,0:T(8,128)S(1)} all-to-all(f32[8,40,128]{2,1,0:T(8,128)S(1)} %get-tuple-element.19), channel_id=1, replica_groups=mesh['y'=8,'z'=8,'c'=2,'x'=4] {'y'}, dimensions={0} | all-to-all | bytes 327680 | tf_op jit(solution)/shard_map/all_to_all | solution.py:392
  78.9 16.6 %all_to_all.29.slices_ref = f32[8,4,40,128]{3,2,1,0:T(8,128)S(1)} all-to-all(f32[8,4,40,128]{3,2,1,0:T(8,128)S(1)} %broadcast_in_dim.5), channel_id=1, replica_groups=mesh['y'=8,'z'=8,'c'=2,'x'=4] {'c','x'}, dimensions={0} | all-to-all | bytes 1310720 | tf_op jit(solution)/shard_map/all_to_all | solution.py:392
  95.5 9.0 %shard_map.71 = (f32[64,2048]{1,0:T(8,128)}, f32[1,3,256,256]{3,2,1,0:T(8,128)}, f32[256,256]{1,0:T(8,128)}) custom-call(f32[8,4,40,128]{3,2,1,0:T(8,128)S(1)} %all_to_all.29.slices_ref, f32[4,2,64,256]{3,2,1,0:T(8,128)S(1)} %shard_map.68.send_ref), custom_call_target="tpu_custom_call" | custom-call | tf_op jit(solution)/shard_map/pallas_call | solution.py:351
  (6 shorter events, 0.1 us)
Async XLA Ops:
  1.7 23.3 %collective-permute-start.1 = (bf16[128,2048]{1,0:T(8,128)(2,1)S(1)}, bf16[128,2048]{1,0:T(8,128)(2,1)S(1)}, u32[]{:S(2)}, u32[]{:S(2)}) collective-permute-start(bf16[128,2048]{1,0:T(8,128)(2,1)S(1)} %pad_maximum_fusion.own_ref), channel_id=1, source_target_pairs={{0,508},{4,8},{8,4},{12,16},{16,12},{20,24},{24,20},{28,32},{32,28... | collective-permute-start | bytes 1572872 | tf_op jit(solution)/shard_map/ppermute | solution.py:405
  7.1 17.9 %collective-permute-start = (bf16[128,2048]{1,0:T(8,128)(2,1)S(1)}, bf16[128,2048]{1,0:T(8,128)(2,1)S(1)}, u32[]{:S(2)}, u32[]{:S(2)}) collective-permute-start(bf16[128,2048]{1,0:T(8,128)(2,1)S(1)} %pad_maximum_fusion.own_ref), channel_id=1, source_target_pairs={{0,4},{4,0},{8,12},{12,8},{16,20},{20,16},{24,28},{28,24},{32,36},... | collective-permute-start | bytes 1572872 | tf_op jit(solution)/shard_map/ppermute | solution.py:406
  18.4 0.7 copy-start
  18.4 0.7 copy-start.1

commit v7 on v6

--- a/solution.py
+++ b/solution.py
@@ -257,17 +257,16 @@
                 pivots[b] = pivot if j == 0 else jnp.where(sub == j, pivot, pivots[b])
                 if j == 7 and s == 3:
                     continue
-                ratio = [
-                    None if l <= j else jnp.broadcast_to(here[l][j:j + 1, :], (8, 128)) * inverse
-                    for l in range(8)
+                across = [
+                    None if l <= j else jnp.broadcast_to(here[l][j:j + 1, :], (8, 128)) for l in range(8)
                 ]
-                row = [jnp.broadcast_to(part[b][s][q][j:j + 1, :], (8, 128)) * inverse for q in lanes]
+                row = [jnp.broadcast_to(part[b][s][q][j:j + 1, :], (8, 128)) for q in lanes]
                 for g in range(s, 4):
                     if g == s and j == 7:
                         continue
-                    c = cols[b][g][j]
+                    c = cols[b][g][j] * inverse
                     for l in range(j + 1, 8):
-                        cols[b][g][l] = cols[b][g][l] - c * ratio[l]
+                        cols[b][g][l] = cols[b][g][l] - c * across[l]
                     if g == s:
                         c = jnp.where(sub > j, c, 0.0)
                     part[b][g] = [part[b][g][q] - c * row[q] for q in lanes]
@@ -302,7 +301,7 @@
                 beside(k)
 
 
-def factor_kernel(scales, slices_ref, send_ref, turned, nodes, root, work, upper, left, right, sems):
+def factor_kernel(scales, base_ref, mine_ref, others_ref, send_ref, turned, nodes, root, slices_ref, work, upper, left, right, sems):
     n = len(scales)
     copies = []
 
@@ -312,12 +311,15 @@
 
     for b in range(BLOCKS):
         copy(send_ref.at[b // 2, b % 2], turned.at[:, pl.ds(BOX * b, BOX)])
+    core = base_ref[0] // BLOCKS % 2
+    slices_ref[core] = mine_ref[...]
+    slices_ref[1 - core] = others_ref[...]
     ri = lax.broadcasted_iota(jnp.int32, (128, 128), 0)
     ci = lax.broadcasted_iota(jnp.int32, (128, 128), 1)
     eye = jnp.where(ri == ci, 1.0, 0.0)
     below = ri >= ci
     for b in range(n):
-        t = jnp.concatenate([slices_ref[r, b] for r in range(8)], axis=0) * scales[b]
+        t = jnp.concatenate([slices_ref[r // 4, r % 4, b] for r in range(8)], axis=0) * scales[b]
         work[b, 0:64, 0:128] = t[0:64] + eye[0:64]
         work[b, 0:64, 128:256] = t[64:128]
         work[b, 64:128, 0:128] = t[256:320] + eye[64:128]
@@ -345,7 +347,7 @@
         c.wait()
 
 
-def factors(slices, send, scales):
+def factors(base, slices, others, send, scales):
     n = len(scales)
     any_place = pl.BlockSpec(memory_space=pl.ANY)
     return pl.pallas_call(
@@ -355,13 +357,13 @@
             jax.ShapeDtypeStruct((1, LEVELS, 256, 256), F),
             jax.ShapeDtypeStruct((256, 256), F),
         ),
-        in_specs=[VM, VM],
+        in_specs=[SM, VM, VM, VM],
         out_specs=(any_place,) * 3,
-        scratch_shapes=[pltpu.VMEM((n, 256, 256), F)] * 2
+        scratch_shapes=[pltpu.VMEM((2,) + slices.shape, F)] + [pltpu.VMEM((n, 256, 256), F)] * 2
         + [pltpu.VMEM((n, 256, 128), F)] * 2
         + [pltpu.SemaphoreType.DMA((BLOCKS + 2 * n,))],
         compiler_params=pltpu.CompilerParams(vmem_limit_bytes=LIMIT),
-    )(slices, send)
+    )(base, slices, others, send)
 
 
 def line_kernel(base_ref, slices, level2, level3, line):
@@ -414,9 +416,10 @@
     level2, level3, line = line_sums(base, along_z)
     along_y = exchange(line, "y")
     root = jnp.sum(along_y, axis=0)
-    slices = to_all(jnp.stack([level1, level2, level3, root]), ("c", "x"), 8)
+    slices = to_all(jnp.stack([level1, level2, level3, root]), "x", 4)
+    others = lax.ppermute(slices, "c", [(0, 1), (1, 0)])
     scales = [1.0 / (rows * 2 ** (l + 1)) for l in range(LEVELS)] + [1.0 / (rows * size)]
-    turned, node_factors, root_factor = factors(slices, send, scales)
+    turned, node_factors, root_factor = factors(base, slices, others, send, scales)
     return turned.T, node_factors, root_factor
 
 

time: 105 us -> 103 us (0.981)
  blocking collectives: 64.9 us -> 53.9 us
  starting transfers between devices: 16.7 us -> 23.4 us
  waiting for transfers between devices: 0.01 us -> 1.06 us
    all_to_all x5, blocking collectives: 64.9 us -> 53.9 us  [exchange(): return lax.all_to_all(x, axes, 0, 0)]
    ppermute x0 -> x1, starting transfers between devices: none -> 6.66 us  [body(): others = lax.ppermute(slices, 'c', [(0, 1), (1, 0)])]
    ppermute x0 -> x1, waiting for transfers between devices: none -> 1.05 us  [body(): others = lax.ppermute(slices, 'c', [(0, 1), (1, 0)])]
  transfers between devices with their start and end apart: 2 -> 3, of which waited for: 0 -> 1; matrix products, arithmetic and copies ran while one was open for 0% -> 0% of each run, Pallas kernels for 6% -> 6%
where the time goes in v7:
time: 103 us; the launch traced here: 102 us
  blocking collectives  53.9 us (52%)
  starting transfers between devices  23.4 us (23%)
  Pallas kernels  20.9 us (20%)
  other arithmetic  1.1 us (1%)
  waiting for transfers between devices  1.06 us (1%)
    all_to_all x5, blocking collectives, exchange(): return lax.all_to_all(x, axes, 0, 0)  53.9 us
    ppermute x1, starting transfers between devices, body(): near = lax.ppermute(packed, leaf, [(i, i ^ 1) for i in range(size)])  11.3 us
    pallas_call x1, Pallas kernels, factors(): pl.pallas_call(functools.partial(factor_kernel, scales), out_shape=(jax.S...  8.88 us
    ppermute x1, starting transfers between devices, body(): others = lax.ppermute(slices, 'c', [(0, 1), (1, 0)])  6.66 us
    pallas_call x1, Pallas kernels, own_tiles(): pl.pallas_call(own_kernel, out_shape=(jax.ShapeDtypeStruct((BLOCKS, 64, B...  5.96 us
    ppermute x1, starting transfers between devices, body(): far = lax.ppermute(packed, leaf, across)  5.39 us
    pallas_call x1, Pallas kernels, halo_tiles(): pl.pallas_call(halo_kernel, out_shape=jax.ShapeDtypeStruct((BLOCKS // 2,...  5.38 us
  transfers between devices with their start and end apart: 3, of which 1 were waited for; matrix products, arithmetic and copies ran while one was open for 0% of the time, Pallas kernels for 6%

profile of v7, /device:TPU:1, one launch (start us, length us, event | category | flops | bytes accessed | tf_op | source)
XLA Modules:
  0.0 102.0 jit_solution(5647201977634822865)
XLA Ops:
  0.6 1.1 %pad_maximum_fusion.own_ref = bf16[128,2048]{1,0:T(8,128)(2,1)S(1)} fusion(bf16[64,2048]{1,0:T(8,128)(2,1)} %bitcast.12, bf16[64,2048]{1,0:T(8,128)(2,1)} %bitcast.13), kind=kLoop, calls=%fused_computation | loop fusion | flops 1048576 | bytes 1048576 | tf_op jit(solution)/shard_map/concatenate | solution.py:405
  1.7 5.4 %collective-permute-start.1 = (bf16[128,2048]{1,0:T(8,128)(2,1)S(1)}, bf16[128,2048]{1,0:T(8,128)(2,1)S(1)}, u32[]{:S(2)}, u32[]{:S(2)}) collective-permute-start(bf16[128,2048]{1,0:T(8,128)(2,1)S(1)} %pad_maximum_fusion.own_ref), channel_id=1, source_target_pairs={{0,508},{4,8},{8,4},{12,16},{16,12},{20,24},{24,20},{28,32},{32,28... | collective-permute-start | bytes 1572872 | tf_op jit(solution)/shard_map/ppermute | solution.py:407
  7.1 11.3 %collective-permute-start = (bf16[128,2048]{1,0:T(8,128)(2,1)S(1)}, bf16[128,2048]{1,0:T(8,128)(2,1)S(1)}, u32[]{:S(2)}, u32[]{:S(2)}) collective-permute-start(bf16[128,2048]{1,0:T(8,128)(2,1)S(1)} %pad_maximum_fusion.own_ref), channel_id=1, source_target_pairs={{0,4},{4,0},{8,12},{12,8},{16,20},{20,16},{24,28},{28,24},{32,36},... | collective-permute-start | bytes 1572872 | tf_op jit(solution)/shard_map/ppermute | solution.py:408
  18.4 0.0 copy-start
  18.4 0.0 copy-start.1
  18.5 0.7 copy-done
  19.1 0.0 copy-done.1
  19.1 6.0 %shard_map.67 = (f32[8,64,256]{2,1,0:T(8,128)S(1)}, bf16[8,128,256]{2,1,0:T(8,128)(2,1)S(1)}, s32[2,152]{1,0:T(2,128)S(1)}, s32[1]{0:T(128)}) custom-call(s32[1]{0:T(128)} %bitcast.base_ref, s32[8,16]{1,0:T(8,128)S(1)} %copy-done, s32[8]{0:T(128)S(1)} %copy-done.1, bf16[128,2048]{1,0:T(8,128)(2,1)S(1)} %pad_maximum_fusion.own_ref), custom_call_target="tpu_custom_call" | custom-call | flops 3221225472 | bytes 4194304 | tf_op jit(solution)/shard_map/pallas_call | solution.py:168
  25.1 0.0 collective-permute-done.1.far_ref
  25.1 0.0 collective-permute-done.near_ref
  25.1 5.4 %shard_map.68.send_ref = f32[4,2,64,256]{3,2,1,0:T(8,128)S(1)} custom-call(s32[2,152]{1,0:T(2,128)S(1)} %get-tuple-element.13.ids, s32[1]{0:T(128)} %get-tuple-element.14.end_ref, bf16[128,2048]{1,0:T(8,128)(2,1)S(1)} %collective-permute-done.near_ref, bf16[128,2048]{1,0:T(8,128)(2,1)S(1)} %collective-permute-done.1.far_ref, ...), custom_call_target="tpu_custom_call" | custom-call | flops 3221225472 | bytes 4194304 | tf_op jit(solution)/shard_map/pallas_call | solution.py:191
  30.5 12.8 %all_to_all.25.columns_ref = f32[4,2,64,256]{3,2,1,0:T(8,128)S(1)} all-to-all(f32[4,2,64,256]{3,2,1,0:T(8,128)S(1)} %shard_map.68.send_ref), channel_id=1, replica_groups=mesh['y'=8,'z'=8,'c'=2,'x'=4] {'x'}, dimensions={0} | all-to-all | bytes 1048576 | tf_op jit(solution)/shard_map/all_to_all | solution.py:394
  43.3 0.7 shard_map.69
  43.9 7.9 %all_to_all.26 = f32[8,40,128]{2,1,0:T(8,128)S(1)} all-to-all(f32[8,40,128]{2,1,0:T(8,128)S(1)} %bitcast.9), channel_id=1, replica_groups=mesh['y'=8,'z'=8,'c'=2,'x'=4] {'c','x'}, dimensions={0} | all-to-all | bytes 327680 | tf_op jit(solution)/shard_map/all_to_all | solution.py:394
  51.9 11.5 %all_to_all.27.slices = f32[8,40,128]{2,1,0:T(8,128)S(1)} all-to-all(f32[8,40,128]{2,1,0:T(8,128)S(1)} %broadcast_in_dim.4), channel_id=1, replica_groups=mesh['y'=8,'z'=8,'c'=2,'x'=4] {'z'}, dimensions={0} | all-to-all | bytes 327680 | tf_op jit(solution)/shard_map/all_to_all | solution.py:394
  63.4 13.4 %all_to_all.28 = f32[8,40,128]{2,1,0:T(8,128)S(1)} all-to-all(f32[8,40,128]{2,1,0:T(8,128)S(1)} %get-tuple-element.19), channel_id=1, replica_groups=mesh['y'=8,'z'=8,'c'=2,'x'=4] {'y'}, dimensions={0} | all-to-all | bytes 327680 | tf_op jit(solution)/shard_map/all_to_all | solution.py:394
  76.9 8.3 %all_to_all.29.mine_ref = f32[4,4,40,128]{3,2,1,0:T(8,128)S(1)} all-to-all(f32[4,4,40,128]{3,2,1,0:T(8,128)S(1)} %broadcast_in_dim.5), channel_id=1, replica_groups=mesh['y'=8,'z'=8,'c'=2,'x'=4] {'x'}, dimensions={0} | all-to-all | bytes 655360 | tf_op jit(solution)/shard_map/all_to_all | solution.py:394
  85.2 6.7 %collective-permute-start.2 = (f32[4,4,40,128]{3,2,1,0:T(8,128)S(1)}, f32[4,4,40,128]{3,2,1,0:T(8,128)S(1)}, u32[]{:S(2)}, u32[]{:S(2)}) collective-permute-start(f32[4,4,40,128]{3,2,1,0:T(8,128)S(1)} %all_to_all.29.mine_ref), channel_id=1, source_target_pairs={{0,4},{4,0},{1,5},{5,1},{2,6},{6,2},{3,7},{7,3},{8,12},{12,8},{9,1... | collective-permute-start | bytes 983048 | tf_op jit(solution)/shard_map/ppermute | solution.py:420
  91.9 1.1 %collective-permute-done.2.others_ref = f32[4,4,40,128]{3,2,1,0:T(8,128)S(1)} collective-permute-done((f32[4,4,40,128]{3,2,1,0:T(8,128)S(1)}, f32[4,4,40,128]{3,2,1,0:T(8,128)S(1)}, u32[]{:S(2)}, u32[]{:S(2)}) %collective-permute-start.2) | collective-permute-done | bytes 327712 | tf_op jit(solution)/shard_map/ppermute | solution.py:420
  92.9 8.9 %shard_map.71 = (f32[64,2048]{1,0:T(8,128)}, f32[1,3,256,256]{3,2,1,0:T(8,128)}, f32[256,256]{1,0:T(8,128)}) custom-call(s32[1]{0:T(128)} %bitcast.base_ref, f32[4,4,40,128]{3,2,1,0:T(8,128)S(1)} %all_to_all.29.mine_ref, f32[4,4,40,128]{3,2,1,0:T(8,128)S(1)} %collective-permute-done.2.others_ref, f32[4,2,64,256]{3,2,1,0:T(8,128)S(1)} %shard_map.68.send_ref), custom_call_target="tpu_custom_call" | custom-call | tf_op jit(solution)/shard_map/pallas_call | solution.py:353
  (6 shorter events, 0.1 us)
Async XLA Ops:
  1.7 23.4 %collective-permute-start.1 = (bf16[128,2048]{1,0:T(8,128)(2,1)S(1)}, bf16[128,2048]{1,0:T(8,128)(2,1)S(1)}, u32[]{:S(2)}, u32[]{:S(2)}) collective-permute-start(bf16[128,2048]{1,0:T(8,128)(2,1)S(1)} %pad_maximum_fusion.own_ref), channel_id=1, source_target_pairs={{0,508},{4,8},{8,4},{12,16},{16,12},{20,24},{24,20},{28,32},{32,28... | collective-permute-start | bytes 1572872 | tf_op jit(solution)/shard_map/ppermute | solution.py:407
  7.1 18.0 %collective-permute-start = (bf16[128,2048]{1,0:T(8,128)(2,1)S(1)}, bf16[128,2048]{1,0:T(8,128)(2,1)S(1)}, u32[]{:S(2)}, u32[]{:S(2)}) collective-permute-start(bf16[128,2048]{1,0:T(8,128)(2,1)S(1)} %pad_maximum_fusion.own_ref), channel_id=1, source_target_pairs={{0,4},{4,0},{8,12},{12,8},{16,20},{20,16},{24,28},{28,24},{32,36},... | collective-permute-start | bytes 1572872 | tf_op jit(solution)/shard_map/ppermute | solution.py:408
  18.4 0.7 copy-start
  18.4 0.7 copy-start.1
  85.2 7.7 %collective-permute-start.2 = (f32[4,4,40,128]{3,2,1,0:T(8,128)S(1)}, f32[4,4,40,128]{3,2,1,0:T(8,128)S(1)}, u32[]{:S(2)}, u32[]{:S(2)}) collective-permute-start(f32[4,4,40,128]{3,2,1,0:T(8,128)S(1)} %all_to_all.29.mine_ref), channel_id=1, source_target_pairs={{0,4},{4,0},{1,5},{5,1},{2,6},{6,2},{3,7},{7,3},{8,12},{12,8},{9,1... | collective-permute-start | bytes 983048 | tf_op jit(solution)/shard_map/ppermute | solution.py:420

commit v8 on v7

--- a/solution.py
+++ b/solution.py
@@ -390,12 +390,47 @@
     )(base, slices)
 
 
+def sum_of(slices):
+    low = (slices[0] + slices[1]) + (slices[2] + slices[3])
+    return low + ((slices[4] + slices[5]) + (slices[6] + slices[7]))
+
+
+def first_kernel(slices, level1, spread):
+    total = sum_of(slices)
+    level1[...] = total
+    for k in range(8):
+        spread[k] = total
+
+
+def last_kernel(slices, level1, level2, level3, spread):
+    levels = (level1[...], level2[...], level3[...], sum_of(slices))
+    for k in range(4):
+        for l, x in enumerate(levels):
+            spread[k, l] = x
+
+
+def first_sums(slices):
+    return pl.pallas_call(
+        first_kernel,
+        out_shape=(jax.ShapeDtypeStruct(slices.shape[1:], F), jax.ShapeDtypeStruct(slices.shape, F)),
+        in_specs=[VM],
+        out_specs=(VM, VM),
+        compiler_params=pltpu.CompilerParams(vmem_limit_bytes=LIMIT),
+    )(slices)
+
+
+def last_sums(slices, level1, level2, level3):
+    return pl.pallas_call(
+        last_kernel,
+        out_shape=jax.ShapeDtypeStruct((4, LEVELS + 1) + slices.shape[1:], F),
+        in_specs=[VM] * 4,
+        out_specs=VM,
+        compiler_params=pltpu.CompilerParams(vmem_limit_bytes=LIMIT),
+    )(slices, level1, level2, level3)
+
+
 def exchange(x, axes):
     return lax.all_to_all(x, axes, 0, 0)
-
-
-def to_all(x, axes, n):
-    return exchange(jnp.broadcast_to(x[None], (n,) + x.shape), axes)
 
 
 def body(points, probes, near_list, near_count):
@@ -411,12 +446,11 @@
     send = halo_tiles(ids, end, near, far, sides, part)
     columns = exchange(send, "x")
     pieces = gram(columns).reshape(8, 40, 128)
-    level1 = jnp.sum(exchange(pieces, ("c", "x")), axis=0)
-    along_z = to_all(level1, "z", 8)
+    level1, spread = first_sums(exchange(pieces, ("c", "x")))
+    along_z = exchange(spread, "z")
     level2, level3, line = line_sums(base, along_z)
     along_y = exchange(line, "y")
-    root = jnp.sum(along_y, axis=0)
-    slices = to_all(jnp.stack([level1, level2, level3, root]), "x", 4)
+    slices = exchange(last_sums(along_y, level1, level2, level3), "x")
     others = lax.ppermute(slices, "c", [(0, 1), (1, 0)])
     scales = [1.0 / (rows * 2 ** (l + 1)) for l in range(LEVELS)] + [1.0 / (rows * size)]
     turned, node_factors, root_factor = factors(base, slices, others, send, scales)

time: 103 us -> 103 us (level)
  no operation moved by 1% of the time
where the time goes in v8:
time: 103 us; the launch traced here: 102 us
  blocking collectives  54.4 us (53%)
  starting transfers between devices  23.4 us (23%)
  Pallas kernels  21 us (20%)
  other arithmetic  1.07 us (1%)
  waiting for transfers between devices  1.06 us (1%)
    all_to_all x5, blocking collectives, exchange(): return lax.all_to_all(x, axes, 0, 0)  54.4 us
    ppermute x1, starting transfers between devices, body(): near = lax.ppermute(packed, leaf, [(i, i ^ 1) for i in range(size)])  11.3 us
    pallas_call x1, Pallas kernels, factors(): pl.pallas_call(functools.partial(factor_kernel, scales), out_shape=(jax.S...  8.88 us
    ppermute x1, starting transfers between devices, body(): others = lax.ppermute(slices, 'c', [(0, 1), (1, 0)])  6.66 us
    pallas_call x1, Pallas kernels, own_tiles(): pl.pallas_call(own_kernel, out_shape=(jax.ShapeDtypeStruct((BLOCKS, 64, B...  5.95 us
    ppermute x1, starting transfers between devices, body(): far = lax.ppermute(packed, leaf, across)  5.39 us
    pallas_call x1, Pallas kernels, halo_tiles(): pl.pallas_call(halo_kernel, out_shape=jax.ShapeDtypeStruct((BLOCKS // 2,...  5.38 us
  transfers between devices with their start and end apart: 3, of which 1 were waited for; matrix products, arithmetic and copies ran while one was open for 0% of the time, Pallas kernels for 6%

profile of v8, /device:TPU:1, one launch (start us, length us, event | category | flops | bytes accessed | tf_op | source)
XLA Modules:
  0.0 102.4 jit_solution(16027628550372718483)
XLA Ops:
  0.6 1.1 %pad_maximum_fusion.own_ref = bf16[128,2048]{1,0:T(8,128)(2,1)S(1)} fusion(bf16[64,2048]{1,0:T(8,128)(2,1)} %bitcast.6, bf16[64,2048]{1,0:T(8,128)(2,1)} %bitcast.7), kind=kLoop, calls=%fused_computation | loop fusion | flops 1048576 | bytes 1048576 | tf_op jit(solution)/shard_map/concatenate | solution.py:440
  1.7 5.4 %collective-permute-start.1 = (bf16[128,2048]{1,0:T(8,128)(2,1)S(1)}, bf16[128,2048]{1,0:T(8,128)(2,1)S(1)}, u32[]{:S(2)}, u32[]{:S(2)}) collective-permute-start(bf16[128,2048]{1,0:T(8,128)(2,1)S(1)} %pad_maximum_fusion.own_ref), channel_id=1, source_target_pairs={{0,508},{4,8},{8,4},{12,16},{16,12},{20,24},{24,20},{28,32},{32,28... | collective-permute-start | bytes 1572872 | tf_op jit(solution)/shard_map/ppermute | solution.py:442
  7.1 11.3 %collective-permute-start = (bf16[128,2048]{1,0:T(8,128)(2,1)S(1)}, bf16[128,2048]{1,0:T(8,128)(2,1)S(1)}, u32[]{:S(2)}, u32[]{:S(2)}) collective-permute-start(bf16[128,2048]{1,0:T(8,128)(2,1)S(1)} %pad_maximum_fusion.own_ref), channel_id=1, source_target_pairs={{0,4},{4,0},{8,12},{12,8},{16,20},{20,16},{24,28},{28,24},{32,36},... | collective-permute-start | bytes 1572872 | tf_op jit(solution)/shard_map/ppermute | solution.py:443
  18.4 0.0 copy-start
  18.4 0.0 copy-start.1
  18.5 0.7 copy-done
  19.1 0.0 copy-done.1
  19.1 6.0 %shard_map.67 = (f32[8,64,256]{2,1,0:T(8,128)S(1)}, bf16[8,128,256]{2,1,0:T(8,128)(2,1)S(1)}, s32[2,152]{1,0:T(2,128)S(1)}, s32[1]{0:T(128)}) custom-call(s32[1]{0:T(128)} %bitcast.base_ref, s32[8,16]{1,0:T(8,128)S(1)} %copy-done, s32[8]{0:T(128)S(1)} %copy-done.1, bf16[128,2048]{1,0:T(8,128)(2,1)S(1)} %pad_maximum_fusion.own_ref), custom_call_target="tpu_custom_call" | custom-call | flops 3221225472 | bytes 4194304 | tf_op jit(solution)/shard_map/pallas_call | solution.py:168
  25.1 0.0 collective-permute-done.1.far_ref
  25.1 0.0 collective-permute-done.near_ref
  25.1 5.4 %shard_map.68.send_ref = f32[4,2,64,256]{3,2,1,0:T(8,128)S(1)} custom-call(s32[2,152]{1,0:T(2,128)S(1)} %get-tuple-element.15.ids, s32[1]{0:T(128)} %get-tuple-element.16.end_ref, bf16[128,2048]{1,0:T(8,128)(2,1)S(1)} %collective-permute-done.near_ref, bf16[128,2048]{1,0:T(8,128)(2,1)S(1)} %collective-permute-done.1.far_ref, ...), custom_call_target="tpu_custom_call" | custom-call | flops 3221225472 | bytes 4194304 | tf_op jit(solution)/shard_map/pallas_call | solution.py:191
  30.5 13.8 %all_to_all.25.columns_ref = f32[4,2,64,256]{3,2,1,0:T(8,128)S(1)} all-to-all(f32[4,2,64,256]{3,2,1,0:T(8,128)S(1)} %shard_map.68.send_ref), channel_id=1, replica_groups=mesh['y'=8,'z'=8,'c'=2,'x'=4] {'x'}, dimensions={0} | all-to-all | bytes 1048576 | tf_op jit(solution)/shard_map/all_to_all | solution.py:433
  44.3 0.7 shard_map.69
  45.0 8.3 %all_to_all.26.slices = f32[8,40,128]{2,1,0:T(8,128)S(1)} all-to-all(f32[8,40,128]{2,1,0:T(8,128)S(1)} %bitcast.5), channel_id=1, replica_groups=mesh['y'=8,'z'=8,'c'=2,'x'=4] {'c','x'}, dimensions={0} | all-to-all | bytes 327680 | tf_op jit(solution)/shard_map/all_to_all | solution.py:433
  53.3 11.5 %all_to_all.27.slices = f32[8,40,128]{2,1,0:T(8,128)S(1)} all-to-all(f32[8,40,128]{2,1,0:T(8,128)S(1)} %get-tuple-element.19), channel_id=1, replica_groups=mesh['y'=8,'z'=8,'c'=2,'x'=4] {'z'}, dimensions={0} | all-to-all | bytes 327680 | tf_op jit(solution)/shard_map/all_to_all | solution.py:433
  64.9 12.5 %all_to_all.28.slices = f32[8,40,128]{2,1,0:T(8,128)S(1)} all-to-all(f32[8,40,128]{2,1,0:T(8,128)S(1)} %get-tuple-element.20), channel_id=1, replica_groups=mesh['y'=8,'z'=8,'c'=2,'x'=4] {'y'}, dimensions={0} | all-to-all | bytes 327680 | tf_op jit(solution)/shard_map/all_to_all | solution.py:433
  77.4 8.3 %all_to_all.29.mine_ref = f32[4,4,40,128]{3,2,1,0:T(8,128)S(1)} all-to-all(f32[4,4,40,128]{3,2,1,0:T(8,128)S(1)} %shard_map.72), channel_id=1, replica_groups=mesh['y'=8,'z'=8,'c'=2,'x'=4] {'x'}, dimensions={0} | all-to-all | bytes 655360 | tf_op jit(solution)/shard_map/all_to_all | solution.py:433
  85.6 6.7 %collective-permute-start.2 = (f32[4,4,40,128]{3,2,1,0:T(8,128)S(1)}, f32[4,4,40,128]{3,2,1,0:T(8,128)S(1)}, u32[]{:S(2)}, u32[]{:S(2)}) collective-permute-start(f32[4,4,40,128]{3,2,1,0:T(8,128)S(1)} %all_to_all.29.mine_ref), channel_id=1, source_target_pairs={{0,4},{4,0},{1,5},{5,1},{2,6},{6,2},{3,7},{7,3},{8,12},{12,8},{9,1... | collective-permute-start | bytes 983048 | tf_op jit(solution)/shard_map/ppermute | solution.py:454
  92.3 1.1 %collective-permute-done.2.others_ref = f32[4,4,40,128]{3,2,1,0:T(8,128)S(1)} collective-permute-done((f32[4,4,40,128]{3,2,1,0:T(8,128)S(1)}, f32[4,4,40,128]{3,2,1,0:T(8,128)S(1)}, u32[]{:S(2)}, u32[]{:S(2)}) %collective-permute-start.2) | collective-permute-done | bytes 327712 | tf_op jit(solution)/shard_map/ppermute | solution.py:454
  93.3 8.9 %shard_map.73 = (f32[64,2048]{1,0:T(8,128)}, f32[1,3,256,256]{3,2,1,0:T(8,128)}, f32[256,256]{1,0:T(8,128)}) custom-call(s32[1]{0:T(128)} %bitcast.base_ref, f32[4,4,40,128]{3,2,1,0:T(8,128)S(1)} %all_to_all.29.mine_ref, f32[4,4,40,128]{3,2,1,0:T(8,128)S(1)} %collective-permute-done.2.others_ref, f32[4,2,64,256]{3,2,1,0:T(8,128)S(1)} %shard_map.68.send_ref), custom_call_target="tpu_custom_call" | custom-call | tf_op jit(solution)/shard_map/pallas_call | solution.py:353
  (3 shorter events, 0.1 us)
Async XLA Ops:
  1.7 23.4 %collective-permute-start.1 = (bf16[128,2048]{1,0:T(8,128)(2,1)S(1)}, bf16[128,2048]{1,0:T(8,128)(2,1)S(1)}, u32[]{:S(2)}, u32[]{:S(2)}) collective-permute-start(bf16[128,2048]{1,0:T(8,128)(2,1)S(1)} %pad_maximum_fusion.own_ref), channel_id=1, source_target_pairs={{0,508},{4,8},{8,4},{12,16},{16,12},{20,24},{24,20},{28,32},{32,28... | collective-permute-start | bytes 1572872 | tf_op jit(solution)/shard_map/ppermute | solution.py:442
  7.1 18.0 %collective-permute-start = (bf16[128,2048]{1,0:T(8,128)(2,1)S(1)}, bf16[128,2048]{1,0:T(8,128)(2,1)S(1)}, u32[]{:S(2)}, u32[]{:S(2)}) collective-permute-start(bf16[128,2048]{1,0:T(8,128)(2,1)S(1)} %pad_maximum_fusion.own_ref), channel_id=1, source_target_pairs={{0,4},{4,0},{8,12},{12,8},{16,20},{20,16},{24,28},{28,24},{32,36},... | collective-permute-start | bytes 1572872 | tf_op jit(solution)/shard_map/ppermute | solution.py:443
  18.4 0.7 copy-start
  18.4 0.7 copy-start.1
  85.6 7.7 %collective-permute-start.2 = (f32[4,4,40,128]{3,2,1,0:T(8,128)S(1)}, f32[4,4,40,128]{3,2,1,0:T(8,128)S(1)}, u32[]{:S(2)}, u32[]{:S(2)}) collective-permute-start(f32[4,4,40,128]{3,2,1,0:T(8,128)S(1)} %all_to_all.29.mine_ref), channel_id=1, source_target_pairs={{0,4},{4,0},{1,5},{5,1},{2,6},{6,2},{3,7},{7,3},{8,12},{12,8},{9,1... | collective-permute-start | bytes 983048 | tf_op jit(solution)/shard_map/ppermute | solution.py:454
